TPU v7x, 128 devices: a whole 4x4x4 slice. The times are simulated.
128 devices in a mesh: batch: 4 (over y), seq: 32 (over z, x, core).
Axes of the slice: x: 4, y: 4, z: 4, core: 2. Of those that a mesh axis runs over, the one named last changes fastest.
Arguments:
- tokens: bfloat16 [2, 4, 8192, 640], P(None, 'batch', 'seq'), may hold values from -6 to 6
- lengths: int32 [2, 4, 64], P(None, 'batch'), may hold values from 1 to 1024, 8192 in all within a row
- gain_one: bfloat16 [640], P('batch'), may hold values from 0.5 to 1.5
- bias_one: bfloat16 [640], P('batch'), may hold values from -3 to 3
- w_qkv: bfloat16 [640, 1920], P('batch'), may hold values from -0.25 to 0.25
- w_out: bfloat16 [640, 640], P('batch'), may hold values from -1 to 1
- gain_two: bfloat16 [640], P('batch'), may hold values from 0.5 to 1.5
- bias_two: bfloat16 [640], P('batch'), may hold values from -3 to 3
- w_up: bfloat16 [640, 5120], P('batch'), may hold values from -0.25 to 0.25
- w_down: bfloat16 [5120, 640], P('batch'), may hold values from -0.078125 to 0.078125
- cotangent: bfloat16 [2, 4, 8192, 640], P(None, 'batch', 'seq'), may hold values from -6 to 6
Outputs:
- block_out: bfloat16 [2, 4, 8192, 640], P(None, 'batch', 'seq')
- grad_tokens: bfloat16 [2, 4, 8192, 640], P(None, 'batch', 'seq')
- grad_gain_one: float32 [640], P('batch')
- grad_bias_one: float32 [640], P('batch')
- grad_qkv: float32 [640, 1920], P('batch')
- grad_out_proj: float32 [640, 640], P('batch')
- grad_gain_two: float32 [640], P('batch')
- grad_bias_two: float32 [640], P('batch')
- grad_up: float32 [640, 5120], P('batch')
- grad_down: float32 [5120, 640], P('batch')
Inputs may be any that keep to these rules, and one draw needn't show every extreme that they name: Each stream's row of 64 lengths sums to 8192; the largest in each row is 1024.
All inputs are finite; a program needn't handle non-finite values.
Results may differ from a plain program's by a relative error of at most 0.029.
Values may be sent and summed in bfloat16 or wider, within the bound.
No kernel may reach another device: no remote copies, remote signals or barrier semaphores. Data moves between devices by JAX's collectives and lax.ppermute only.
A program may use at most 192 MiB of HBM per device.

v0:
```python
import jax
import jax.numpy as jnp
from jax import lax
from jax.sharding import PartitionSpec as P

HEADS = 20
MAXLEN = 1024


epsilon = 1e-05
group_width = 4


def passed_along(array, axis, by):
    devices = lax.axis_size(axis)
    pairs = [(i, i + by) for i in range(devices) if 0 <= i + by < devices]
    return lax.ppermute(array, axis, pairs)


def layer_norm(vector, gain, shift):
    average = jnp.mean(vector, axis=-1, keepdims=True)
    centred = vector - average
    spread = jnp.mean(centred * centred, axis=-1, keepdims=True)
    return centred * lax.rsqrt(spread + epsilon) * gain + shift


def gelu_exact(vector):
    return jax.nn.gelu(vector, approximate=False)


def segment_of(places, length_row):
    boundaries = jnp.cumsum(length_row)
    return jnp.sum((places[:, None] >= boundaries[None, :]).astype(jnp.int32), axis=1)


def split_groups(tensor, group_count):
    tok_rows = tensor.shape[0]
    return tensor.reshape(tok_rows, group_count, group_width, -1).transpose(1, 0, 2, 3)


def join_groups(tensor):
    tok_rows = tensor.shape[1]
    return tensor.transpose(1, 0, 2, 3).reshape(tok_rows, -1)


def body(
    tokens, lengths, gain_one, bias_one, w_qkv, w_out, gain_two, bias_two, w_up, w_down, cotangent
):
    gain_one, bias_one, w_qkv, w_out, gain_two, bias_two, w_up, w_down = (
        lax.all_gather(gain_one, "batch", axis=0, tiled=True),
        lax.all_gather(bias_one, "batch", axis=0, tiled=True),
        lax.all_gather(w_qkv, "batch", axis=0, tiled=True),
        lax.all_gather(w_out, "batch", axis=0, tiled=True),
        lax.all_gather(gain_two, "batch", axis=0, tiled=True),
        lax.all_gather(bias_two, "batch", axis=0, tiled=True),
        lax.all_gather(w_up, "batch", axis=0, tiled=True),
        lax.all_gather(w_down, "batch", axis=0, tiled=True),
    )
    model_width = w_qkv.shape[0]
    head_dim = model_width // HEADS
    groups = HEADS // group_width
    score_scale = head_dim ** (-0.5)
    tok_rows = tokens.shape[2]
    devices = lax.axis_size("seq")
    reach_blocks = min((MAXLEN - 1) // tok_rows + 1, devices - 1)
    stream_rows = tok_rows * devices
    local_places = lax.axis_index("seq") * tok_rows + jnp.arange(tok_rows, dtype=jnp.int32)
    offsets = list(range(reach_blocks, -reach_blocks - 1, -1))
    key_places = jnp.concatenate([local_places - offset * tok_rows for offset in offsets])
    in_stream = (key_places >= 0) & (key_places < stream_rows)
    gain_f1 = gain_one.astype(jnp.float32)
    bias_f1 = bias_one.astype(jnp.float32)
    gain_f2 = gain_two.astype(jnp.float32)
    bias_f2 = bias_two.astype(jnp.float32)
    acc_gain_one = jnp.zeros(gain_f1.shape, jnp.float32)
    acc_bias_one = jnp.zeros(gain_f1.shape, jnp.float32)
    acc_gain_two = jnp.zeros(gain_f1.shape, jnp.float32)
    acc_bias_two = jnp.zeros(gain_f1.shape, jnp.float32)
    acc_qkv = jnp.zeros(w_qkv.shape, jnp.float32)
    acc_out = jnp.zeros(w_out.shape, jnp.float32)
    acc_up = jnp.zeros(w_up.shape, jnp.float32)
    acc_down = jnp.zeros(w_down.shape, jnp.float32)
    outputs = []
    grad_inputs = []
    for micro_step in range(tokens.shape[0]):
        length_row = lengths[micro_step, 0]
        query_segment = segment_of(local_places, length_row)
        key_segment = segment_of(key_places, length_row)
        allowed = (query_segment[:, None] == key_segment[None, :]) & in_stream[None, :]
        inputs = tokens[micro_step, 0].astype(jnp.float32)
        normed_one, pull_one = jax.vjp(layer_norm, inputs, gain_f1, bias_f1)
        hidden_one = normed_one.astype(jnp.bfloat16)
        projected = jnp.dot(hidden_one, w_qkv, preferred_element_type=jnp.float32).astype(
            jnp.bfloat16
        )
        queries = projected[:, :model_width]
        key_value = projected[:, model_width:]
        pieces = []
        for offset in offsets:
            if offset == 0:
                pieces.append(key_value)
            else:
                pieces.append(passed_along(key_value, "seq", offset))
        window = jnp.concatenate(pieces, axis=0)
        query_groups = split_groups(queries, groups)
        key_groups = split_groups(window[:, :model_width], groups)
        value_groups = split_groups(window[:, model_width:], groups)

        def attend(operands):
            query_block, key_block, value_block = operands
            scores = (
                jnp.einsum(
                    "qhd,khd->hqk", query_block, key_block, preferred_element_type=jnp.float32
                )
                * score_scale
            )
            scores = jnp.where(allowed[None], scores, -1e30)
            largest = jnp.max(scores, axis=-1, keepdims=True)
            raised = jnp.exp(scores - largest)
            totals = jnp.sum(raised, axis=-1, keepdims=True)
            attn_weights = (raised / totals).astype(jnp.bfloat16)
            mixed = jnp.einsum(
                "hqk,khd->qhd", attn_weights, value_block, preferred_element_type=jnp.float32
            )
            return (mixed, (largest + jnp.log(totals))[..., 0])

        mixed_groups, log_totals = lax.map(attend, (query_groups, key_groups, value_groups))
        attended = join_groups(mixed_groups)
        attended_low = attended.astype(jnp.bfloat16)
        middle = inputs + jnp.dot(attended_low, w_out, preferred_element_type=jnp.float32)
        normed_two, pull_two = jax.vjp(layer_norm, middle, gain_f2, bias_f2)
        hidden_two = normed_two.astype(jnp.bfloat16)
        upward = jnp.dot(hidden_two, w_up, preferred_element_type=jnp.float32)
        activated, pull_gelu = jax.vjp(gelu_exact, upward)
        activated_low = activated.astype(jnp.bfloat16)
        result = middle + jnp.dot(activated_low, w_down, preferred_element_type=jnp.float32)
        outputs.append(result.astype(jnp.bfloat16))
        grad_result = cotangent[micro_step, 0]
        acc_down = acc_down + jnp.einsum(
            "tf,td->fd", activated_low, grad_result, preferred_element_type=jnp.float32
        )
        grad_activated = jnp.einsum(
            "td,fd->tf", grad_result, w_down, preferred_element_type=jnp.float32
        )
        grad_upward = pull_gelu(grad_activated)[0].astype(jnp.bfloat16)
        acc_up = acc_up + jnp.einsum(
            "tc,tf->cf", hidden_two, grad_upward, preferred_element_type=jnp.float32
        )
        grad_hidden_two = jnp.einsum(
            "tf,cf->tc", grad_upward, w_up, preferred_element_type=jnp.float32
        )
        grad_mid_part, grad_g2, grad_b2 = pull_two(grad_hidden_two)
        acc_gain_two = acc_gain_two + grad_g2
        acc_bias_two = acc_bias_two + grad_b2
        grad_middle = grad_result.astype(jnp.float32) + grad_mid_part
        grad_branch = grad_middle.astype(jnp.bfloat16)
        acc_out = acc_out + jnp.einsum(
            "tc,td->cd", attended_low, grad_branch, preferred_element_type=jnp.float32
        )
        grad_attended = jnp.einsum(
            "td,cd->tc", grad_branch, w_out, preferred_element_type=jnp.float32
        ).astype(jnp.bfloat16)
        delta_rows = jnp.sum(
            (grad_attended.astype(jnp.float32) * attended).reshape(tok_rows, HEADS, head_dim),
            axis=-1,
        )
        delta_groups = delta_rows.reshape(tok_rows, groups, group_width).transpose(1, 2, 0)
        grad_groups = split_groups(grad_attended, groups)

        def attend_back(operands):
            query_block, key_block, value_block, grad_block, log_block, delta_block = operands
            scores = (
                jnp.einsum(
                    "qhd,khd->hqk", query_block, key_block, preferred_element_type=jnp.float32
                )
                * score_scale
            )
            scores = jnp.where(allowed[None], scores, -1e30)
            attn_weights = jnp.exp(scores - log_block[..., None])
            grad_weights = jnp.einsum(
                "qhd,khd->hqk", grad_block, value_block, preferred_element_type=jnp.float32
            )
            grad_scores = (attn_weights * (grad_weights - delta_block[..., None])).astype(
                jnp.bfloat16
            )
            grad_query = (
                jnp.einsum(
                    "hqk,khd->qhd", grad_scores, key_block, preferred_element_type=jnp.float32
                )
                * score_scale
            )
            grad_key = (
                jnp.einsum(
                    "hqk,qhd->khd", grad_scores, query_block, preferred_element_type=jnp.float32
                )
                * score_scale
            )
            grad_value = jnp.einsum(
                "hqk,qhd->khd",
                attn_weights.astype(jnp.bfloat16),
                grad_block,
                preferred_element_type=jnp.float32,
            )
            return (grad_query, grad_key, grad_value)

        grad_q_groups, grad_k_groups, grad_v_groups = lax.map(
            attend_back,
            (query_groups, key_groups, value_groups, grad_groups, log_totals, delta_groups),
        )
        grad_window = jnp.concatenate(
            [join_groups(grad_k_groups), join_groups(grad_v_groups)], axis=1
        )
        grad_key_value = jnp.zeros((tok_rows, 2 * model_width), jnp.float32)
        for position, offset in enumerate(offsets):
            piece = grad_window[position * tok_rows : (position + 1) * tok_rows]
            if offset == 0:
                grad_key_value = grad_key_value + piece
            else:
                grad_key_value = grad_key_value + passed_along(
                    piece.astype(jnp.bfloat16), "seq", -offset
                ).astype(piece.dtype)
        grad_projected = jnp.concatenate(
            [join_groups(grad_q_groups), grad_key_value], axis=1
        ).astype(jnp.bfloat16)
        acc_qkv = acc_qkv + jnp.einsum(
            "tc,te->ce", hidden_one, grad_projected, preferred_element_type=jnp.float32
        )
        grad_hidden_one = jnp.einsum(
            "te,ce->tc", grad_projected, w_qkv, preferred_element_type=jnp.float32
        )
        grad_in_part, grad_g1, grad_b1 = pull_one(grad_hidden_one)
        acc_gain_one = acc_gain_one + grad_g1
        acc_bias_one = acc_bias_one + grad_b1
        grad_inputs.append((grad_middle + grad_in_part).astype(jnp.bfloat16))
    gradients = (
        acc_gain_one,
        acc_bias_one,
        acc_qkv,
        acc_out,
        acc_gain_two,
        acc_bias_two,
        acc_up,
        acc_down,
    )
    summed = (
        lax.psum(gradients[0].astype(jnp.bfloat16), "seq").astype(jnp.float32),
        lax.psum(gradients[1].astype(jnp.bfloat16), "seq").astype(jnp.float32),
        lax.psum(gradients[2].astype(jnp.bfloat16), "seq").astype(jnp.float32),
        lax.psum(gradients[3].astype(jnp.bfloat16), "seq").astype(jnp.float32),
        lax.psum(gradients[4].astype(jnp.bfloat16), "seq").astype(jnp.float32),
        lax.psum(gradients[5].astype(jnp.bfloat16), "seq").astype(jnp.float32),
        lax.psum(gradients[6].astype(jnp.bfloat16), "seq").astype(jnp.float32),
        lax.psum(gradients[7].astype(jnp.bfloat16), "seq").astype(jnp.float32),
    )
    shares = (
        lax.psum_scatter(
            summed[0].astype(jnp.bfloat16), "batch", scatter_dimension=0, tiled=True
        ).astype(jnp.float32),
        lax.psum_scatter(
            summed[1].astype(jnp.bfloat16), "batch", scatter_dimension=0, tiled=True
        ).astype(jnp.float32),
        lax.psum_scatter(
            summed[2].astype(jnp.bfloat16), "batch", scatter_dimension=0, tiled=True
        ).astype(jnp.float32),
        lax.psum_scatter(
            summed[3].astype(jnp.bfloat16), "batch", scatter_dimension=0, tiled=True
        ).astype(jnp.float32),
        lax.psum_scatter(
            summed[4].astype(jnp.bfloat16), "batch", scatter_dimension=0, tiled=True
        ).astype(jnp.float32),
        lax.psum_scatter(
            summed[5].astype(jnp.bfloat16), "batch", scatter_dimension=0, tiled=True
        ).astype(jnp.float32),
        lax.psum_scatter(
            summed[6].astype(jnp.bfloat16), "batch", scatter_dimension=0, tiled=True
        ).astype(jnp.float32),
        lax.psum_scatter(
            summed[7].astype(jnp.bfloat16), "batch", scatter_dimension=0, tiled=True
        ).astype(jnp.float32),
    )
    return (
        jnp.stack(outputs)[:, None],
        jnp.stack(grad_inputs)[:, None],
        shares[0],
        shares[1],
        shares[2],
        shares[3],
        shares[4],
        shares[5],
        shares[6],
        shares[7],
    )


def solution(mesh):
    return jax.shard_map(
        body,
        mesh=mesh,
        in_specs=(
            P(None, "batch", "seq", None),
            P(None, "batch", None),
            P("batch"),
            P("batch"),
            P("batch", None),
            P("batch", None),
            P("batch"),
            P("batch"),
            P("batch", None),
            P("batch", None),
            P(None, "batch", "seq", None),
        ),
        out_specs=(
            P(None, "batch", "seq", None),
            P(None, "batch", "seq", None),
            P("batch"),
            P("batch"),
            P("batch", None),
            P("batch", None),
            P("batch"),
            P("batch"),
            P("batch", None),
            P("batch", None),
        ),
        check_vma=False,
    )
```

profile of v0, /device:TPU:1, one launch (start us, length us, event | category | flops | bytes accessed | tf_op | source)
XLA Modules:
  0.0 1041.0 jit_solution(3484337336710424782)
XLA Ops:
  10.4 14.5 %all_gather.27 = bf16[640,640]{1,0:T(8,128)(2,1)} all-gather(bf16[160,640]{1,0:T(8,128)(2,1)} %param.24), channel_id=1, replica_groups=mesh['batch'=4,'seq'=32] {'batch'}, dimensions={0}, use_global_device_ids=true | all-gather | bytes 1024000 | tf_op jit(solution)/shard_map/all_gather | solution.py:53
  38.0 9.9 all-gather.4.cloned.1.call-done
  85.7 11.6 %collective-permute-done.10 = bf16[256,1280]{1,0:T(8,128)(2,1)} collective-permute-done((bf16[256,1280]{1,0:T(8,128)(2,1)S(1)}, bf16[256,1280]{1,0:T(8,128)(2,1)}, u32[]{:S(2)}, u32[]{:S(2)}) %collective-permute-start.10) | collective-permute-done | bytes 655392 | tf_op jit(solution)/shard_map/ppermute | solution.py:17
  105.2 10.1 collective-permute-start
  116.5 10.0 collective-permute-start.1
  145.9 51.6 %while.57 = (s32[]{:T(128)}, f32[5,256,4,32]{1,3,2,0:T(8,128)}, f32[5,4,256]{2,1,0:T(4,128)S(1)}, bf16[5,2304,4,32]{1,3,2,0:T(8,128)(2,1)}, bf16[5,256,4,32]{1,3...) while((s32[]{:T(128)}, f32[5,256,4,32]{1,3,2,0:T(8,128)}, ...), condition=%wide.region_19.20_spmd.clone, body=%wide.region_16.19_spmd.clone.sunk | while | flops 331480064 | bytes 32094576 | solution.py:127
  207.4 8.9 collective-permute-done.5
  237.8 47.4 %while.56 = (s32[]{:T(128)}, f32[5,256,4,32]{1,3,2,0:T(8,128)}, f32[5,4,256]{2,1,0:T(4,128)S(1)}, bf16[5,2304,4,32]{1,3,2,0:T(8,128)(2,1)}, bf16[5,256,4,32]{1,3...) while((s32[]{:T(128)}, f32[5,256,4,32]{1,3,2,0:T(8,128)}, ...), condition=%wide.region_8.9_spmd.clone, body=%wide.region_5.8_spmd.clone.sunk | while | flops 331480064 | bytes 32094576 | solution.py:127
  296.4 16.6 %multiply_convert_fusion.2 = (bf16[256,5120]{1,0:T(8,128)(2,1)}, f32[256,5120]{1,0:T(8,128)}, f32[256,5120]{1,0:T(8,128)}) fusion(bf16[640,5120]{1,0:T(8,128)(2,1)} %all-gather.6.cloned.1.call-done, f32[256,640]{1,0:T(8,128)} %copy-done.5, f32[256]{0:T(256)S(1)} %fusion.198, f32[256]{0:T(256)S(1)} %broadcast_multiply_fusion, f32[640]{0:T(1024)S(1)} %copy-done.51, ...), kind=kOutput, calls=%fused_computation.138 | convolution fusion | flops 1763737600 | bytes 20323328 | tf_op jit(solution)/shard_map/dot_general | solution.py:133
  313.0 17.1 %multiply_convert_fusion.3 = (bf16[256,5120]{1,0:T(8,128)(2,1)}, f32[256,5120]{1,0:T(8,128)}, f32[256,5120]{1,0:T(8,128)}) fusion(bf16[640,5120]{1,0:T(8,128)(2,1)S(1)} %copy-done.94, f32[256,640]{1,0:T(8,128)S(1)} %copy-done.9, f32[640]{0:T(1024)S(1)} %copy-done.51, f32[640]{0:T(1024)S(1)} %copy-done.49, f32[256]{0:T(256)S(1)} %fusion.196, ...), kind=kOutput, calls=%fused_computation.151 | convolution fusion | flops 1763737600 | bytes 20323328 | tf_op jit(solution)/shard_map/dot_general | solution.py:133
  330.2 9.1 add_convert_fusion.2
  367.9 86.4 %while.59 = (s32[]{:T(128)}, bf16[5,256,4,32]{1,3,2,0:T(8,128)(2,1)S(1)}, f32[5,2304,4,32]{1,3,2,0:T(8,128)}, f32[5,2304,4,32]{1,3,2,0:T(8,128)}, bf16[5,2304,4,...) while((s32[]{:T(128)}, ...), condition=%wide.region_33.34_spmd.clone, body=%wide.region_32.33_spmd.clone.sunk | while | flops 780075008 | bytes 48805264 | solution.py:206
  474.5 9.8 collective-permute-start.30
  484.4 17.7 %collective-permute-start.29 = (bf16[256,1280]{0,1:T(8,128)(2,1)}, bf16[256,1280]{0,1:T(8,128)(2,1)}, u32[]{:S(2)}, u32[]{:S(2)}) collective-permute-start(bf16[256,1280]{0,1:T(8,128)(2,1)} %get-tuple-element.509), channel_id=1, source_target_pairs={{0,2},{1,3},{2,4},{3,5},{4,6},{5,7},{6,8},{7,9},{8,10},{9,11},{10,... | collective-permute-start | bytes 1966088 | tf_op jit(solution)/shard_map/ppermute | solution.py:17
  509.6 89.2 %while.58 = (s32[]{:T(128)}, bf16[5,256,4,32]{1,3,2,0:T(8,128)(2,1)}, f32[5,2304,4,32]{1,3,2,0:T(8,128)}, f32[5,2304,4,32]{1,3,2,0:T(8,128)}, bf16[5,2304,4,32]{...) while((s32[]{:T(128)}, ...), condition=%wide.region_26.27_spmd.clone, body=%wide.region_25.26_spmd.clone.sunk | while | flops 780075008 | bytes 48805264 | solution.py:206
  631.7 12.8 %collective-permute-done.22 = bf16[256,1280]{0,1:T(8,128)(2,1)S(1)} collective-permute-done((bf16[256,1280]{0,1:T(8,128)(2,1)S(1)}, bf16[256,1280]{0,1:T(8,128)(2,1)S(1)}, u32[]{:S(2)}, u32[]{:S(2)}) %collective-permute-start.22) | collective-permute-done | bytes 655392 | tf_op jit(solution)/shard_map/ppermute | solution.py:17
  645.8 10.1 collective-permute-done.21
  674.5 13.1 %collective-permute-done.16 = bf16[256,1280]{0,1:T(8,128)(2,1)} collective-permute-done((bf16[256,1280]{0,1:T(8,128)(2,1)}, bf16[256,1280]{0,1:T(8,128)(2,1)}, u32[]{:S(2)}, u32[]{:S(2)}) %collective-permute-start.16) | collective-permute-done | bytes 655392 | tf_op jit(solution)/shard_map/ppermute | solution.py:17
  701.3 14.3 %collective-permute-done.24 = bf16[256,1280]{0,1:T(8,128)(2,1)S(1)} collective-permute-done((bf16[256,1280]{0,1:T(8,128)(2,1)}, bf16[256,1280]{0,1:T(8,128)(2,1)S(1)}, u32[]{:S(2)}, u32[]{:S(2)}) %collective-permute-start.24) | collective-permute-done | bytes 655392 | tf_op jit(solution)/shard_map/ppermute | solution.py:17
  755.2 17.2 %reduce-scatter.5.cloned.1.call-done = bf16[160,1920]{1,0:T(8,128)(2,1)} async-done(((bf16[640,1920]{1,0:T(8,128)(2,1)}), bf16[160,1920]{1,0:T(8,128)(2,1)}) %reduce-scatter.5.cloned.1.call-update) | async-done | bytes 614416 | tf_op jit(solution)/shard_map/reduce_scatter | solution.py:262
  772.4 68.1 %reduce-scatter.9.cloned.1.call-done = bf16[160,5120]{1,0:T(8,128)(2,1)} async-done(((bf16[640,5120]{1,0:T(8,128)(2,1)}), bf16[160,5120]{1,0:T(8,128)(2,1)}) %reduce-scatter.9.cloned.1.call-update) | async-done | bytes 1638416 | tf_op jit(solution)/shard_map/reduce_scatter | solution.py:274
  840.5 68.3 %reduce-scatter.11.cloned.1.call-done = bf16[1280,640]{1,0:T(8,128)(2,1)} async-done(((bf16[5120,640]{1,0:T(8,128)(2,1)}), bf16[1280,640]{1,0:T(8,128)(2,1)}) %reduce-scatter.11.cloned.1.call-update) | async-done | bytes 1638416 | tf_op jit(solution)/shard_map/reduce_scatter | solution.py:277
  920.1 65.0 %all-reduce.8 = (bf16[160]{0:T(256)(128)(2,1)S(1)}, bf16[160]{0:T(256)(128)(2,1)S(1)}, bf16[160]{0:T(256)(128)(2,1)S(1)}, bf16[160]{0:T(256)(128)(2,1)S(1)}) all-reduce(bf16[160]{0:T(256)(128)(2,1)S(1)} %dynamic-slice.5, bf16[160]{0:T(256)(128)(2,1)S(1)} %dynamic-slice.7, ...), channel_id=1, replica_groups=mesh['batch'=4,'seq'=32] {'seq'}, use_global_device_ids=true, to_apply=%region_38.39 | all-reduce | flops 640 | bytes 2560 | tf_op jit(solution)/shard_map/psum | solution.py:246
  990.1 34.4 %all-reduce.14.cloned.1.call-done = (bf16[160,1920]{1,0:T(8,128)(2,1)}, bf16[160,640]{1,0:T(8,128)(2,1)}, bf16[160,5120]{1,0:T(8,128)(2,1)}, bf16[1280,640]{1,0:T(8,128)(2,1)}) async-done(((bf16[160,1920]{1,0:T(8,128)(2,1)}, bf16[160,640]{1,0:T(8,128)(2,1)}, bf16[160,5120]{1,0:T(8,128)(2,1)}, bf16[1280,640]{1,0:T(8,128)(2,1)}), (bf16[160,1920]{1,0:T(8,128)(2,1)}, bf16[160,640]{1,0:T(8,128)(2,1)}, ...) | async-done | bytes 4096016 | tf_op jit(solution)/shard_map/psum | solution.py:248
  (553 shorter events, 584.0 us)
Async XLA Ops:
  7.3 40.7 %all-gather.4.cloned.1.call-start = ((), (), s32[]{:S(2)}) async-start(), calls=%async_computation.4 | async-start | bytes 3072000 | tf_op jit(solution)/shard_map/all_gather | solution.py:52
  8.0 288.4 %all-gather.6.cloned.1.call-start = ((), (), s32[]{:S(2)}) async-start(), calls=%async_computation.5 | async-start | bytes 8192000 | tf_op jit(solution)/shard_map/all_gather | solution.py:56
  8.7 321.4 %all-gather.8.cloned.1.call-start = ((), (), s32[]{:S(2)}) async-start(), calls=%async_computation.6 | async-start | bytes 8192000 | tf_op jit(solution)/shard_map/all_gather | solution.py:57
  9.5 745.7 %reduce-scatter.7.cloned.1.call-start = ((), (), s32[]{:S(2)}) async-start(), calls=%async_computation.8 | async-start | bytes 1024000 | tf_op jit(solution)/shard_map/reduce_scatter | solution.py:265
  63.6 41.6 %collective-permute-start.11 = (bf16[256,1280]{1,0:T(8,128)(2,1)S(1)}, bf16[256,1280]{1,0:T(8,128)(2,1)}, u32[]{:S(2)}, u32[]{:S(2)}) collective-permute-start(bf16[256,1280]{1,0:T(8,128)(2,1)S(1)} %slice.148), channel_id=1, source_target_pairs={{0,1},{1,2},{2,3},{3,4},{4,5},{5,6},{6,7},{7,8},{8,9},{9,10},{10,1... | collective-permute-start | bytes 1966088 | tf_op jit(solution)/shard_map/ppermute | solution.py:17
  65.5 51.0 %collective-permute-start.12 = (bf16[256,1280]{1,0:T(8,128)(2,1)S(1)}, bf16[256,1280]{1,0:T(8,128)(2,1)}, u32[]{:S(2)}, u32[]{:S(2)}) collective-permute-start(bf16[256,1280]{1,0:T(8,128)(2,1)S(1)} %slice.148), channel_id=1, source_target_pairs={{1,0},{2,1},{3,2},{4,3},{5,4},{6,5},{7,6},{8,7},{9,8},{10,9},{11,1... | collective-permute-start | bytes 1966088 | tf_op jit(solution)/shard_map/ppermute | solution.py:17
  72.1 55.5 %collective-permute-start.13 = (bf16[256,1280]{1,0:T(8,128)(2,1)S(1)}, bf16[256,1280]{1,0:T(8,128)(2,1)S(1)}, u32[]{:S(2)}, u32[]{:S(2)}) collective-permute-start(bf16[256,1280]{1,0:T(8,128)(2,1)S(1)} %slice.148), channel_id=1, source_target_pairs={{2,0},{3,1},{4,2},{5,3},{6,4},{7,5},{8,6},{9,7},{10,8},{11,9},{12,... | collective-permute-start | bytes 1966088 | tf_op jit(solution)/shard_map/ppermute | solution.py:17
  83.2 46.7 %collective-permute-start.14 = (bf16[256,1280]{1,0:T(8,128)(2,1)S(1)}, bf16[256,1280]{1,0:T(8,128)(2,1)S(1)}, u32[]{:S(2)}, u32[]{:S(2)}) collective-permute-start(bf16[256,1280]{1,0:T(8,128)(2,1)S(1)} %slice.148), channel_id=1, source_target_pairs={{3,0},{4,1},{5,2},{6,3},{7,4},{8,5},{9,6},{10,7},{11,8},{12,9},{13... | collective-permute-start | bytes 1966088 | tf_op jit(solution)/shard_map/ppermute | solution.py:17
  105.2 92.3 %collective-permute-start = (bf16[256,1280]{1,0:T(8,128)(2,1)}, bf16[256,1280]{1,0:T(8,128)(2,1)}, u32[]{:S(2)}, u32[]{:S(2)}) collective-permute-start(bf16[256,1280]{1,0:T(8,128)(2,1)} %slice.144), channel_id=1, source_target_pairs={{0,4},{1,5},{2,6},{3,7},{4,8},{5,9},{6,10},{7,11},{8,12},{9,13},{1... | collective-permute-start | bytes 1966088 | tf_op jit(solution)/shard_map/ppermute | solution.py:17
  116.5 83.6 %collective-permute-start.1 = (bf16[256,1280]{1,0:T(8,128)(2,1)}, bf16[256,1280]{1,0:T(8,128)(2,1)}, u32[]{:S(2)}, u32[]{:S(2)}) collective-permute-start(bf16[256,1280]{1,0:T(8,128)(2,1)} %slice.144), channel_id=1, source_target_pairs={{0,3},{1,4},{2,5},{3,6},{4,7},{5,8},{6,9},{7,10},{8,11},{9,12},{10... | collective-permute-start | bytes 1966088 | tf_op jit(solution)/shard_map/ppermute | solution.py:17
  127.7 75.0 %collective-permute-start.2 = (bf16[256,1280]{1,0:T(8,128)(2,1)}, bf16[256,1280]{1,0:T(8,128)(2,1)}, u32[]{:S(2)}, u32[]{:S(2)}) collective-permute-start(bf16[256,1280]{1,0:T(8,128)(2,1)} %slice.144), channel_id=1, source_target_pairs={{0,2},{1,3},{2,4},{3,5},{4,6},{5,7},{6,8},{7,9},{8,10},{9,11},{10,... | collective-permute-start | bytes 1966088 | tf_op jit(solution)/shard_map/ppermute | solution.py:17
  129.9 75.2 %collective-permute-start.3 = (bf16[256,1280]{1,0:T(8,128)(2,1)}, bf16[256,1280]{1,0:T(8,128)(2,1)}, u32[]{:S(2)}, u32[]{:S(2)}) collective-permute-start(bf16[256,1280]{1,0:T(8,128)(2,1)} %slice.144), channel_id=1, source_target_pairs={{0,1},{1,2},{2,3},{3,4},{4,5},{5,6},{6,7},{7,8},{8,9},{9,10},{10,1... | collective-permute-start | bytes 1966088 | tf_op jit(solution)/shard_map/ppermute | solution.py:17
  131.9 74.4 %collective-permute-start.4 = (bf16[256,1280]{1,0:T(8,128)(2,1)}, bf16[256,1280]{1,0:T(8,128)(2,1)}, u32[]{:S(2)}, u32[]{:S(2)}) collective-permute-start(bf16[256,1280]{1,0:T(8,128)(2,1)} %slice.144), channel_id=1, source_target_pairs={{1,0},{2,1},{3,2},{4,3},{5,4},{6,5},{7,6},{8,7},{9,8},{10,9},{11,1... | collective-permute-start | bytes 1966088 | tf_op jit(solution)/shard_map/ppermute | solution.py:17
  466.8 150.9 %collective-permute-start.31 = (bf16[256,1280]{0,1:T(8,128)(2,1)}, bf16[256,1280]{0,1:T(8,128)(2,1)}, u32[]{:S(2)}, u32[]{:S(2)}) collective-permute-start(bf16[256,1280]{0,1:T(8,128)(2,1)} %get-tuple-element.507), channel_id=1, source_target_pairs={{0,4},{1,5},{2,6},{3,7},{4,8},{5,9},{6,10},{7,11},{8,12},{9,13},{1... | collective-permute-start | bytes 1966088 | tf_op jit(solution)/shard_map/ppermute | solution.py:17
  474.5 145.6 %collective-permute-start.30 = (bf16[256,1280]{0,1:T(8,128)(2,1)}, bf16[256,1280]{0,1:T(8,128)(2,1)}, u32[]{:S(2)}, u32[]{:S(2)}) collective-permute-start(bf16[256,1280]{0,1:T(8,128)(2,1)} %get-tuple-element.508), channel_id=1, source_target_pairs={{0,3},{1,4},{2,5},{3,6},{4,7},{5,8},{6,9},{7,10},{8,11},{9,12},{10... | collective-permute-start | bytes 1966088 | tf_op jit(solution)/shard_map/ppermute | solution.py:17
  484.4 138.3 %collective-permute-start.29 = (bf16[256,1280]{0,1:T(8,128)(2,1)}, bf16[256,1280]{0,1:T(8,128)(2,1)}, u32[]{:S(2)}, u32[]{:S(2)}) collective-permute-start(bf16[256,1280]{0,1:T(8,128)(2,1)} %get-tuple-element.509), channel_id=1, source_target_pairs={{0,2},{1,3},{2,4},{3,5},{4,6},{5,7},{6,8},{7,9},{8,10},{9,11},{10,... | collective-permute-start | bytes 1966088 | tf_op jit(solution)/shard_map/ppermute | solution.py:17
  617.7 38.2 %collective-permute-start.21 = (bf16[256,1280]{0,1:T(8,128)(2,1)S(1)}, bf16[256,1280]{0,1:T(8,128)(2,1)S(1)}, u32[]{:S(2)}, u32[]{:S(2)}) collective-permute-start(bf16[256,1280]{0,1:T(8,128)(2,1)S(1)} %get-tuple-element.517), channel_id=1, source_target_pairs={{0,2},{1,3},{2,4},{3,5},{4,6},{5,7},{6,8},{7,9},{8,10},{9,11},{10,... | collective-permute-start | bytes 1966088 | tf_op jit(solution)/shard_map/ppermute | solution.py:17
  620.1 42.9 %collective-permute-start.20 = (bf16[256,1280]{0,1:T(8,128)(2,1)}, bf16[256,1280]{0,1:T(8,128)(2,1)}, u32[]{:S(2)}, u32[]{:S(2)}) collective-permute-start(bf16[256,1280]{0,1:T(8,128)(2,1)} %get-tuple-element.518), channel_id=1, source_target_pairs={{0,1},{1,2},{2,3},{3,4},{4,5},{5,6},{6,7},{7,8},{8,9},{9,10},{10,1... | collective-permute-start | bytes 1966088 | tf_op jit(solution)/shard_map/ppermute | solution.py:17
  622.7 47.0 %collective-permute-start.19 = (bf16[256,1280]{0,1:T(8,128)(2,1)}, bf16[256,1280]{0,1:T(8,128)(2,1)}, u32[]{:S(2)}, u32[]{:S(2)}) collective-permute-start(bf16[256,1280]{0,1:T(8,128)(2,1)} %get-tuple-element.519), channel_id=1, source_target_pairs={{1,0},{2,1},{3,2},{4,3},{5,4},{6,5},{7,6},{8,7},{9,8},{10,9},{11,1... | collective-permute-start | bytes 1966088 | tf_op jit(solution)/shard_map/ppermute | solution.py:17
  630.5 41.2 %collective-permute-start.18 = (bf16[256,1280]{0,1:T(8,128)(2,1)}, bf16[256,1280]{0,1:T(8,128)(2,1)}, u32[]{:S(2)}, u32[]{:S(2)}) collective-permute-start(bf16[256,1280]{0,1:T(8,128)(2,1)} %get-tuple-element.520), channel_id=1, source_target_pairs={{2,0},{3,1},{4,2},{5,3},{6,4},{7,5},{8,6},{9,7},{10,8},{11,9},{12,... | collective-permute-start | bytes 1966088 | tf_op jit(solution)/shard_map/ppermute | solution.py:17
  659.4 113.0 %reduce-scatter.5.cloned.1.call-start = ((), (), s32[]{:S(2)}) async-start(), calls=%async_computation.7 | async-start | bytes 3072000 | tf_op jit(solution)/shard_map/reduce_scatter | solution.py:262
  720.7 119.9 %reduce-scatter.9.cloned.1.call-start = ((), (), s32[]{:S(2)}) async-start(), calls=%async_computation.9 | async-start | bytes 8192000 | tf_op jit(solution)/shard_map/reduce_scatter | solution.py:274
  729.6 179.2 %reduce-scatter.11.cloned.1.call-start = ((), (), s32[]{:S(2)}) async-start(), calls=%async_computation.10 | async-start | bytes 8192000 | tf_op jit(solution)/shard_map/reduce_scatter | solution.py:277
  739.9 284.6 %all-reduce.14.cloned.1.call-start = ((), (), s32[]{:S(2)}) async-start(), calls=%async_computation.11 | async-start | bytes 8192000 | tf_op jit(solution)/shard_map/psum | solution.py:248
  (119 other events, 2594.6 us)
Sparse Core Ops, SparseCore 0:
  9.7 38.1 all-gather.3
  49.6 67.8 all-gather.5
  119.2 68.5 all-gather.7
  659.5 37.5 reduce-scatter.6
  720.7 51.6 reduce-scatter.4
  774.7 65.8 reduce-scatter.8
  842.9 65.8 reduce-scatter.10
  912.6 111.8 all-reduce.13
where the time goes:
time: 1050 us; the launch traced here: 1040 us
  matrix products  344 us (33%)
  waiting for transfers between devices  309 us (29%)
  starting transfers between devices  121 us (12%)
  blocking collectives  94.2 us (9%)
  local copies, waits for them, and re-layouts  79.4 us (8%)
  other arithmetic  75.2 us (7%)
  between operations  17.7 us (2%)
    ppermute x32, starting transfers between devices, passed_along(): return lax.ppermute(array, axis, pairs)  120 us
    ppermute x32, waiting for transfers between devices, passed_along(): return lax.ppermute(array, axis, pairs)  109 us
    reduce_scatter x1, waiting for transfers between devices, body(): lax.psum_scatter(summed[7].astype(jnp.bfloat16), 'batch', scatter_dimensi...  68.3 us
    reduce_scatter x1, waiting for transfers between devices, body(): lax.psum_scatter(summed[6].astype(jnp.bfloat16), 'batch', scatter_dimensi...  68.1 us
    psum x1, blocking collectives, body(): lax.psum(gradients[0].astype(jnp.bfloat16), 'seq').astype(jnp.float32)  65 us
    dot_general x10, matrix products, attend_back(): jnp.einsum('qhd,khd->hqk', grad_block, value_block, preferred_element_typ...  46.8 us
    dot_general x10, matrix products, attend(): jnp.einsum('hqk,khd->qhd', attn_weights, value_block, preferred_element_t...  44.7 us
    dot_general x10, matrix products, attend_back(): jnp.einsum('hqk,qhd->khd', attn_weights.astype(jnp.bfloat16), grad_block,...  35.3 us
  transfers between devices with their start and end apart: 40, of which 19 were waited for; matrix products, arithmetic and copies ran while one was open for 34% of the time, Pallas kernels for 0%

commit v1 on v0

v1 whole, which is shorter than its diff:
```python
import math

import jax
import jax.numpy as jnp
from jax import lax
from jax.experimental import pallas as pl
from jax.experimental.pallas import tpu as pltpu
from jax.sharding import Mesh
from jax.sharding import PartitionSpec as P

HEAD_DIM = 32
SCALE = HEAD_DIM ** -0.5
LOG2E = math.log2(math.e)
C2 = SCALE * LOG2E
BIG = 1e30
TILE = 256
EPSILON = 1e-05
PAIRS = 5
SHORT, LONG = 640, 1152
f32, bf16 = jnp.float32, jnp.bfloat16


def pair_offset(info_ref):
    p = pl.program_id(0)
    sub = jnp.where(p == PAIRS - 1, info_ref[0], lax.rem(p, 2))
    return sub * (2 * HEAD_DIM)


def split3(v):
    a = v.astype(bf16)
    r = v - a.astype(f32)
    b = r.astype(bf16)
    d = (r - b.astype(f32)).astype(bf16)
    return a, b, d


def rows_masked(xT, off):
    row = lax.broadcasted_iota(jnp.int32, xT.shape, 0) - off
    xf = xT.astype(f32)
    return [jnp.where((row >= HEAD_DIM * j) & (row < HEAD_DIM * (j + 1)), xf, 0.0).astype(bf16) for j in range(2)]


def lanes_masked(x, off):
    lane = lax.broadcasted_iota(jnp.int32, x.shape, 1) - off
    xf = x.astype(f32)
    return [jnp.where((lane >= HEAD_DIM * j) & (lane < HEAD_DIM * (j + 1)), xf, 0.0).astype(bf16) for j in range(2)]


def attend_kernel(info_ref, qT_ref, k_ref, vT_ref, kaug_ref, qaugT_ref, oT_ref, o_ref, l_ref, rhs):
    off = pair_offset(info_ref)
    oT_ref[...] = jnp.where(lax.rem(pl.program_id(0), 2) == 0, 0.0, oT_ref[...])
    for t in range(2):
        cols = slice(t * TILE, (t + 1) * TILE)
        masked = rows_masked(qT_ref[:, cols], off)
        for j in range(2):
            rhs[0:128, j * TILE:(j + 1) * TILE] = masked[j]
            rhs[128:256, j * TILE:(j + 1) * TILE] = qaugT_ref[:, cols]
        start = info_ref[1 + t]
        need = info_ref[3 + t]

        def block(size):
            def step(i, carry):
                row = pl.multiple_of(start + i * size, 128)
                lhs = jnp.concatenate([k_ref[pl.ds(row, size), :], kaug_ref[pl.ds(row, size), :]], axis=1)
                raw = [jnp.dot(lhs, rhs[:, j * TILE:(j + 1) * TILE], preferred_element_type=f32) for j in range(2)]
                out = []
                for j in range(2):
                    m, l, o = carry[j]
                    s = raw[j] * C2
                    m_new = jnp.maximum(m, jnp.max(s, axis=0, keepdims=True))
                    alpha = jnp.exp2(m - m_new)
                    p = jnp.exp2(s - m_new)
                    vT = vT_ref[pl.ds(pl.multiple_of(off + j * HEAD_DIM, HEAD_DIM), HEAD_DIM), pl.ds(row, size)]
                    out.append((m_new, l * alpha + jnp.sum(p, axis=0, keepdims=True),
                                o * alpha + jnp.dot(vT, p.astype(bf16), preferred_element_type=f32)))
                return tuple(out)
            return step

        def finish(state):
            for j in range(2):
                m, l, o = state[j]
                oT_ref[pl.ds(pl.multiple_of(off + j * HEAD_DIM, HEAD_DIM), HEAD_DIM), cols] = o * (1.0 / l)
                l_ref[0, j:j + 1, cols] = m + jnp.log2(l)

        init = tuple((jnp.full((1, TILE), -1e38, f32), jnp.zeros((1, TILE), f32), jnp.zeros((HEAD_DIM, TILE), f32)) for _ in range(2))

        @pl.when(need <= SHORT)
        def _():
            finish(block(SHORT)(0, init))

        @pl.when(need > SHORT)
        def _():
            finish(lax.fori_loop(0, lax.div(need + (LONG - 1), LONG), block(LONG), init))

    o_ref[...] = oT_ref[...].T.astype(bf16)


def attend(info, qT, k, vT, kaug, qaugT):
    win = k.shape[0]
    nq = qT.shape[1]
    group = lambda p, *_: p // 2
    return pl.pallas_call(
        attend_kernel,
        out_shape=(jax.ShapeDtypeStruct((384, nq), f32), jax.ShapeDtypeStruct((nq, 384), bf16), jax.ShapeDtypeStruct((PAIRS, 8, nq), f32)),
        grid_spec=pltpu.PrefetchScalarGridSpec(
            num_scalar_prefetch=1, grid=(PAIRS,),
            in_specs=[
                pl.BlockSpec((128, nq), lambda p, *_: (p // 2, 0)),
                pl.BlockSpec((win, 128), lambda p, *_: (0, p // 2)),
                pl.BlockSpec((128, win), lambda p, *_: (p // 2, 0)),
                pl.BlockSpec((win, 128), lambda p, *_: (0, 0)),
                pl.BlockSpec((128, nq), lambda p, *_: (0, 0)),
            ],
            out_specs=[
                pl.BlockSpec((128, nq), lambda p, *_: (p // 2, 0)),
                pl.BlockSpec((nq, 128), lambda p, *_: (0, p // 2)),
                pl.BlockSpec((1, 8, nq), lambda p, *_: (p, 0, 0)),
            ],
            scratch_shapes=[pltpu.VMEM((256, 2 * TILE), bf16)],
        ),
        compiler_params=pltpu.CompilerParams(vmem_limit_bytes=48 << 20),
        cost_estimate=pl.CostEstimate(flops=20 * 10**9, bytes_accessed=6 << 20, transcendentals=5 * 10**6),
        name="attend",
    )(info, qT, k, vT, kaug, qaugT)


def attend_back_kernel(info_ref, qT_ref, q_ref, k_ref, kT_ref, v_ref, doT_ref, do_ref, oT_ref, l_ref, kaug_ref, qaugT_ref,
                       dq_ref, dk_ref, dv_ref, dqT_ref, rhs_s, rhs_d, q_stk, do_stk, dk_acc, dv_acc):
    p_id = pl.program_id(0)
    off = pair_offset(info_ref)

    @pl.when(lax.rem(p_id, 2) == 0)
    def _():
        dqT_ref[...] = jnp.zeros_like(dqT_ref)
        dk_acc[...] = jnp.zeros_like(dk_acc)
        dv_acc[...] = jnp.zeros_like(dv_acc)

    for t in range(2):
        cols = slice(t * TILE, (t + 1) * TILE)
        masked_q = rows_masked(qT_ref[:, cols], off)
        masked_do = rows_masked(doT_ref[:, cols], off)
        lane_q = lanes_masked(q_ref[cols, :], off)
        lane_do = lanes_masked(do_ref[cols, :], off)
        for j in range(2):
            part = slice(j * TILE, (j + 1) * TILE)
            head = pl.ds(pl.multiple_of(off + j * HEAD_DIM, HEAD_DIM), HEAD_DIM)
            delta = jnp.sum(doT_ref[head, cols].astype(f32) * oT_ref[head, cols], axis=0, keepdims=True)
            total = l_ref[0, j:j + 1, cols] * (1.0 / C2)
            rowid = lax.broadcasted_iota(jnp.int32, (64, TILE), 0)
            lp, dp = split3(-total), split3(-delta)
            def pieces(parts):
                x = jnp.zeros((64, TILE), f32)
                for n in range(3):
                    x = jnp.where(rowid == n, parts[n].astype(f32), x)
                return x.astype(bf16)
            rhs_s[0:128, part] = masked_q[j]
            rhs_s[128:192, part] = qaugT_ref[0:64, cols]
            rhs_s[192:256, part] = pieces(lp)
            rhs_d[0:128, part] = masked_do[j]
            rhs_d[128:192, part] = jnp.zeros((64, TILE), bf16)
            rhs_d[192:256, part] = pieces(dp)
            q_stk[part, :] = lane_q[j]
            do_stk[part, :] = lane_do[j]
        start = info_ref[1 + t]
        need = info_ref[3 + t]

        def block(size):
            def step(i, carry):
                row = pl.multiple_of(start + i * size, 128)
                rows = pl.ds(row, size)
                aug = kaug_ref[rows, :]
                lhs_k = jnp.concatenate([k_ref[rows, :], aug], axis=1)
                lhs_v = jnp.concatenate([v_ref[rows, :], aug], axis=1)
                out, dv, dk = [], dv_acc[rows, :], dk_acc[rows, :]
                for j in range(2):
                    part = slice(j * TILE, (j + 1) * TILE)
                    s = jnp.dot(lhs_k, rhs_s[:, part], preferred_element_type=f32)
                    dp = jnp.dot(lhs_v, rhs_d[:, part], preferred_element_type=f32)
                    p = jnp.exp2(s * C2)
                    ds = (p * dp).astype(bf16)
                    dv = dv + jnp.dot(p.astype(bf16), do_stk[part, :], preferred_element_type=f32)
                    dk = dk + jnp.dot(ds, q_stk[part, :], preferred_element_type=f32)
                    kT = kT_ref[pl.ds(pl.multiple_of(off + j * HEAD_DIM, HEAD_DIM), HEAD_DIM), rows]
                    out.append(carry[j] + jnp.dot(kT, ds, preferred_element_type=f32))
                dv_acc[rows, :] = dv
                dk_acc[rows, :] = dk
                return tuple(out)
            return step

        def finish(dqs):
            for j in range(2):
                dqT_ref[pl.ds(pl.multiple_of(off + j * HEAD_DIM, HEAD_DIM), HEAD_DIM), cols] = dqs[j] * SCALE

        init = tuple(jnp.zeros((HEAD_DIM, TILE), f32) for _ in range(2))

        @pl.when(need <= SHORT)
        def _():
            finish(block(SHORT)(0, init))

        @pl.when(need > SHORT)
        def _():
            finish(lax.fori_loop(0, lax.div(need + (LONG - 1), LONG), block(LONG), init))
    @pl.when((lax.rem(p_id, 2) == 1) | (p_id == PAIRS - 1))
    def _():
        dq_ref[...] = dqT_ref[...].T.astype(bf16)
        dk_ref[...] = (dk_acc[...] * SCALE).astype(bf16)
        dv_ref[...] = dv_acc[...].astype(bf16)


def attend_back(info, qT, q, k, kT, v, doT, do, oT, lse, kaug, qaugT):
    win, nq = k.shape[0], qT.shape[1]
    wide = pl.BlockSpec((128, nq), lambda p, *_: (p // 2, 0))
    tall = pl.BlockSpec((nq, 128), lambda p, *_: (0, p // 2))
    keys = pl.BlockSpec((win, 128), lambda p, *_: (0, p // 2))
    return pl.pallas_call(
        attend_back_kernel,
        out_shape=(jax.ShapeDtypeStruct((nq, 384), bf16), jax.ShapeDtypeStruct((win, 384), bf16), jax.ShapeDtypeStruct((win, 384), bf16)),
        grid_spec=pltpu.PrefetchScalarGridSpec(
            num_scalar_prefetch=1, grid=(PAIRS,),
            in_specs=[wide, tall, keys, pl.BlockSpec((128, win), lambda p, *_: (p // 2, 0)), keys, wide, tall, wide,
                      pl.BlockSpec((1, 8, nq), lambda p, *_: (p, 0, 0)),
                      pl.BlockSpec((win, 128), lambda p, *_: (0, 0)), pl.BlockSpec((128, nq), lambda p, *_: (0, 0))],
            out_specs=[tall, keys, keys],
            scratch_shapes=[pltpu.VMEM((128, nq), f32), pltpu.VMEM((256, 2 * TILE), bf16), pltpu.VMEM((256, 2 * TILE), bf16),
                            pltpu.VMEM((2 * TILE, 128), bf16), pltpu.VMEM((2 * TILE, 128), bf16),
                            pltpu.VMEM((win, 128), f32), pltpu.VMEM((win, 128), f32)],
        ),
        compiler_params=pltpu.CompilerParams(vmem_limit_bytes=48 << 20),
        cost_estimate=pl.CostEstimate(flops=40 * 10**9, bytes_accessed=12 << 20, transcendentals=5 * 10**6),
        name="attend_back",
    )(info, qT, q, k, kT, v, doT, do, oT, lse, kaug, qaugT)


def qkv_kernel(core_ref, own_ref, other_ref, gain_ref, bias_ref, w_ref, k_ref, v_ref, kT_ref, vT_ref, q_ref, qT_ref, hid_ref):
    block = pl.program_id(0)
    mine = lax.rem(block, 2) == core_ref[0]
    x = jnp.where(mine, own_ref[0].astype(f32), other_ref[0].astype(f32))
    centred = x - jnp.mean(x, axis=-1, keepdims=True)
    spread = jnp.mean(centred * centred, axis=-1, keepdims=True)
    hidden = (centred * lax.rsqrt(spread + EPSILON) * gain_ref[...] + bias_ref[...]).astype(bf16)
    kv = jnp.dot(hidden, w_ref[:, 384:], preferred_element_type=f32).astype(bf16)
    k_ref[...] = kv[:, :384]
    v_ref[...] = kv[:, 384:]
    kvT = kv.astype(f32).T.astype(bf16)
    kT_ref[...] = kvT[:384]
    vT_ref[...] = kvT[384:]

    @pl.when((block == 4) | (block == 5))
    def _():
        q = jnp.dot(hidden, w_ref[:, :384], preferred_element_type=f32).astype(bf16)
        q_ref[...] = q
        qT_ref[...] = q.astype(f32).T.astype(bf16)
        hid_ref[...] = hidden


def project(core, own, other, gain, bias, w):
    rows = 256
    blocks = 2 * own.shape[0]
    win, nq = blocks * rows, 2 * rows
    centre = lambda b: jnp.clip(b - 4, 0, 1)
    return pl.pallas_call(
        qkv_kernel,
        out_shape=(
            jax.ShapeDtypeStruct((win, 384), bf16), jax.ShapeDtypeStruct((win, 384), bf16),
            jax.ShapeDtypeStruct((384, win), bf16), jax.ShapeDtypeStruct((384, win), bf16),
            jax.ShapeDtypeStruct((nq, 384), bf16), jax.ShapeDtypeStruct((384, nq), bf16),
            jax.ShapeDtypeStruct((nq, 640), bf16)),
        grid_spec=pltpu.PrefetchScalarGridSpec(
            num_scalar_prefetch=1, grid=(blocks,),
            in_specs=[
                pl.BlockSpec((1, rows, 640), lambda b, *_: (b // 2, 0, 0)),
                pl.BlockSpec((1, rows, 640), lambda b, *_: (b // 2, 0, 0)),
                pl.BlockSpec((1, 640), lambda b, *_: (0, 0)),
                pl.BlockSpec((1, 640), lambda b, *_: (0, 0)),
                pl.BlockSpec((640, 1152), lambda b, *_: (0, 0)),
            ],
            out_specs=[
                pl.BlockSpec((rows, 384), lambda b, *_: (b, 0)),
                pl.BlockSpec((rows, 384), lambda b, *_: (b, 0)),
                pl.BlockSpec((384, rows), lambda b, *_: (0, b)),
                pl.BlockSpec((384, rows), lambda b, *_: (0, b)),
                pl.BlockSpec((rows, 384), lambda b, *_: (centre(b), 0)),
                pl.BlockSpec((384, rows), lambda b, *_: (0, centre(b))),
                pl.BlockSpec((rows, 640), lambda b, *_: (centre(b), 0)),
            ],
        ),
        compiler_params=pltpu.CompilerParams(vmem_limit_bytes=48 << 20),
        cost_estimate=pl.CostEstimate(flops=5 * 10**9, bytes_accessed=12 << 20, transcendentals=10**4),
        name="project",
    )(core, own, other, gain, bias, w)


def feed_kernel(h_ref, cot_ref, up_ref, down_ref, out_ref, dh_ref, g_up_ref, g_down_ref, hT, cT):
    chunk = pl.program_id(0)

    @pl.when(chunk == 0)
    def _():
        hT[...] = h_ref[...].astype(f32).T.astype(bf16)
        cT[...] = cot_ref[...].astype(f32).T.astype(bf16)
        out_ref[...] = jnp.zeros_like(out_ref)
        dh_ref[...] = jnp.zeros_like(dh_ref)

    nt = (((1,), (1,)), ((), ()))
    h, cot = h_ref[...], cot_ref[...]
    up_w, down_w = up_ref[...], down_ref[...]
    u = jnp.dot(h, up_w, preferred_element_type=f32)
    d_act = lax.dot_general(cot, down_w, nt, preferred_element_type=f32)
    cdf = 0.5 * (1.0 + lax.erf(u * (2.0 ** -0.5)))
    pdf = jnp.exp(u * u * -0.5) * ((2.0 * math.pi) ** -0.5)
    act = (u * cdf).astype(bf16)
    d_up = (d_act * (cdf + u * pdf)).astype(bf16)
    out_ref[...] += jnp.dot(act, down_w, preferred_element_type=f32)
    dh_ref[...] += lax.dot_general(d_up, up_w, nt, preferred_element_type=f32)
    g_up = jnp.dot(hT[...], d_up, preferred_element_type=f32).astype(bf16)
    for y in range(4):
        g_up_ref[y] = g_up[160 * y:160 * (y + 1)]
    g_down_ref[0] = jnp.dot(cT[...], act, preferred_element_type=f32).T.astype(bf16)


def feed_forward(h, cot, up, down):
    rows, chunks, wide = h.shape[0], 4, up.shape[1] // 4
    whole = pl.BlockSpec((rows, 640), lambda f: (0, 0))
    return pl.pallas_call(
        feed_kernel,
        out_shape=(
            jax.ShapeDtypeStruct((rows, 640), f32), jax.ShapeDtypeStruct((rows, 640), f32),
            jax.ShapeDtypeStruct((4, 160 * chunks, wide), bf16), jax.ShapeDtypeStruct((4, wide, 640), bf16)),
        grid=(chunks,),
        in_specs=[whole, whole, pl.BlockSpec((640, wide), lambda f: (0, f)), pl.BlockSpec((wide, 640), lambda f: (f, 0))],
        out_specs=[whole, whole, pl.BlockSpec((4, 160, wide), lambda f: (0, f, 0)), pl.BlockSpec((1, wide, 640), lambda f: (f, 0, 0))],
        scratch_shapes=[pltpu.VMEM((640, rows), bf16), pltpu.VMEM((640, rows), bf16)],
        compiler_params=pltpu.CompilerParams(vmem_limit_bytes=56 << 20),
        cost_estimate=pl.CostEstimate(flops=20 * 10**9, bytes_accessed=30 << 20, transcendentals=5 * 10**6),
        name="feed_forward",
    )(h, cot, up, down)


def moments(x):
    centred = x - jnp.mean(x, axis=-1, keepdims=True)
    r = lax.rsqrt(jnp.mean(centred * centred, axis=-1, keepdims=True) + EPSILON)
    return centred * r, r


def norm_back(grad, n, r, gain):
    e = grad * gain
    return r * (e - jnp.mean(e, axis=-1, keepdims=True) - n * jnp.mean(e * n, axis=-1, keepdims=True))


def shifted(array, axis, by):
    devices = lax.axis_size(axis)
    return lax.ppermute(array, axis, [(i, (i + by) % devices) for i in range(devices)])


def passed_along(array, by):
    devices = lax.axis_size(("z", "x"))
    return lax.ppermute(array, ("z", "x"), [(i, i + by) for i in range(devices) if 0 <= i + by < devices])


def swapped(array):
    return lax.ppermute(array, "core", [(0, 1), (1, 0)])


def pick(array, index):
    return lax.dynamic_index_in_dim(array, index, 0, keepdims=False)


def summed_share(array, axis):
    me, devices = lax.axis_index(axis), lax.axis_size(axis)
    total = pick(array, me).astype(f32)
    for by in (1, devices - 1, 2):
        total = total + shifted(pick(array, (me + by) % devices), axis, by).astype(f32)
    return total.astype(bf16)


def gathered(array, axis):
    me, devices = lax.axis_index(axis), lax.axis_size(axis)
    out = jnp.zeros((devices,) + array.shape, array.dtype)
    out = lax.dynamic_update_index_in_dim(out, array, me, 0)
    for by in (1, devices - 1, 2):
        out = lax.dynamic_update_index_in_dim(out, shifted(array, axis, by), (me + devices - by) % devices, 0)
    return out


def summed_over_chips(array):
    rows = array.shape[0]
    part = summed_share(array.reshape(4, rows // 4, 640), "z")
    part = summed_share(part.reshape(4, rows // 16, 640), "x")
    return gathered(gathered(part, "x").reshape(rows // 4, 640), "z").reshape(rows, 640)


def in_order(core, mine, theirs, axis):
    first = jnp.where(core == 0, mine, theirs)
    second = jnp.where(core == 0, theirs, mine)
    return jnp.concatenate([first, second], axis=axis)


def window_info(length_row, chip, core, win):
    ends = jnp.cumsum(length_row)
    starts = ends - length_row
    base = chip * 512 - 1024
    places = base + jnp.arange(win, dtype=jnp.int32)
    inside = (places[:, None] >= starts[None, :]) & (places[:, None] < ends[None, :])
    ones = jnp.broadcast_to(jnp.arange(64) < 3, (win, 64)).astype(bf16)
    key_rows = jnp.concatenate([jnp.where(inside, 0.0, -BIG).astype(bf16), ones], axis=1)
    own = chip * 512 + jnp.arange(512, dtype=jnp.int32)
    inside_q = (own[None, :] >= starts[:, None]) & (own[None, :] < ends[:, None])
    query_rows = jnp.concatenate([inside_q.astype(bf16), jnp.zeros((64, 512), bf16)], axis=0)
    info = [core]
    sizes = []
    for t in range(2):
        first = chip * 512 + t * TILE
        low = jnp.max(jnp.where(starts <= first, starts, 0)) - base
        high = jnp.min(jnp.where(ends > first + TILE - 1, ends, 1 << 30)) - base
        start = low // 128 * 128
        need = high - start
        size = jnp.where(need <= SHORT, SHORT, (need + LONG - 1) // LONG * LONG)
        info.append(jnp.minimum(start, win - size))
        sizes.append(size)
    return jnp.stack(info + sizes).astype(jnp.int32), key_rows, query_rows


def body(tokens, lengths, gain_one, bias_one, w_qkv, w_out, gain_two, bias_two, w_up, w_down, cotangent):
    core, chip = lax.axis_index("core"), lax.axis_index(("z", "x"))
    tiles = lambda w, axis, base: jnp.concatenate(
        [lax.dynamic_slice_in_dim(w, base + 256 * core, 256, axis), lax.slice_in_dim(w, base + 512, base + 640, axis=axis)], axis=axis)

    vectors = jnp.stack([gain_one, bias_one, gain_two, bias_two], axis=1)
    packed = jnp.concatenate(
        [tiles(w_qkv, 1, 0), tiles(w_qkv, 1, 640), tiles(w_qkv, 1, 1280), w_out, jnp.pad(vectors, ((0, 0), (0, 124)))], axis=1)
    packed = gathered(packed, "batch").reshape(640, -1)
    w_heads, w_out_all = packed[:, :1152], packed[:, 1152:1792]
    gain_f1, bias_f1, gain_f2, bias_f2 = (packed[:, 1792 + i].astype(f32)[None, :] for i in range(4))
    up_half = lax.dynamic_index_in_dim(w_up.reshape(160, 4, 2, 640), core, 2, keepdims=False).reshape(160, 2560)
    up_half = lax.all_gather(up_half, "batch", axis=0, tiled=True)
    down_half = lax.all_gather(lax.dynamic_slice_in_dim(w_down, 640 * core, 640, 0), "batch", axis=0, tiled=True)

    core_arg = core[None].astype(jnp.int32)
    projected = []
    for m in range(2):
        own = tokens[m, 0]
        reach = jnp.stack([passed_along(own, 2), passed_along(own, 1), own, passed_along(own, -1), passed_along(own, -2)])
        projected.append(project(core_arg, reach, swapped(reach), gain_f1, bias_f1, w_heads))
    forward = []
    for m in range(2):
        k, v, kT, vT, q, qT, hidden = projected[m]
        info, key_rows, query_rows = window_info(lengths[m, 0], chip, core, k.shape[0])
        forward.append((info, key_rows, query_rows) + tuple(attend(info, qT, k, vT, key_rows, query_rows)))

    low = jnp.stack([f[4] for f in forward])
    mine = lax.dynamic_slice_in_dim(low, 256 * core, 256, 1)
    theirs = swapped(lax.dynamic_slice_in_dim(low, 256 - 256 * core, 256, 1))
    head_a, head_b = jnp.where(core == 0, mine, theirs), jnp.where(core == 0, theirs, mine)
    attended = jnp.concatenate([head_a[..., :256], head_b[..., :256], head_a[..., 256:] + head_b[..., 256:]], axis=-1).reshape(512, 640)
    inputs = tokens[:, 0].reshape(512, 640).astype(f32)
    middle = inputs + jnp.dot(attended, w_out_all, preferred_element_type=f32)
    n_two, r_two = moments(middle)
    hidden_two = (n_two * gain_f2 + bias_f2).astype(bf16)
    cot = cotangent[:, 0].reshape(512, 640)
    both = swapped(jnp.stack([hidden_two, cot]))
    out, d_hidden, g_up, g_down = feed_forward(
        jnp.concatenate([hidden_two, both[0]]), jnp.concatenate([cot, both[1]]), up_half, down_half)
    back = swapped(jnp.stack([out[512:], d_hidden[512:]]).astype(bf16)).astype(f32)
    block_out = (middle + out[:512] + back[0]).astype(bf16)
    d_hidden = d_hidden[:512] + back[1]
    g_gain_two, g_bias_two = jnp.sum(d_hidden * n_two, axis=0), jnp.sum(d_hidden, axis=0)
    grad_middle = cot.astype(f32) + norm_back(d_hidden, n_two, r_two, gain_f2)
    branch = grad_middle.astype(bf16)
    g_out = lax.dot_general(attended, branch, (((0,), (0,)), ((), ())), preferred_element_type=f32).astype(bf16)
    first = jnp.concatenate([g_up, g_down, g_out.reshape(4, 160, 640)], axis=1)
    first = lax.psum_scatter(first, "batch", scatter_dimension=0, tiled=True).reshape(-1, 640)

    branch_all = in_order(core, branch.reshape(2, 256, 640), swapped(branch).reshape(2, 256, 640), 1)
    w_out_half = tiles(w_out_all, 0, 0)
    nt = (((1,), (1,)), ((), ()))
    grads_kv, grads_q = [], []
    for m in range(2):
        k, v, kT, vT, q, qT, hidden = projected[m]
        info, key_rows, query_rows, oT, _, lse = forward[m]
        do = lax.dot_general(branch_all[m], w_out_half, nt, preferred_element_type=f32).astype(bf16)
        doT = lax.dot_general(w_out_half, branch_all[m], nt, preferred_element_type=f32).astype(bf16)
        dq, dk, dv = attend_back(info, qT, q, k, kT, v, doT, do, oT, lse, key_rows, query_rows)
        pieces = jnp.concatenate([dk, dv], axis=1).reshape(5, 512, 768)
        grads_kv.append(pieces[2].astype(f32) + sum(passed_along(pieces[2 + by], by).astype(f32) for by in (1, -1, 2, -2)))
        grads_q.append(dq)
    grad_projected = jnp.concatenate([jnp.stack(grads_q), jnp.stack(grads_kv).astype(bf16)], axis=2)
    flat = grad_projected.reshape(1024, 1152)
    hidden_all = jnp.concatenate([projected[0][6], projected[1][6]])
    g_qkv = lax.dot_general(hidden_all, flat, (((0,), (0,)), ((), ())), preferred_element_type=f32).astype(bf16)
    d_one = lax.dot_general(flat, w_heads, nt, preferred_element_type=f32).reshape(2, 512, 640)
    d_one = lax.dynamic_slice_in_dim(d_one, 256 * core, 256, 1) + swapped(
        lax.dynamic_slice_in_dim(d_one, 256 - 256 * core, 256, 1).astype(bf16)).astype(f32)
    d_one = d_one.reshape(512, 640)
    n_one, r_one = moments(inputs)
    g_gain_one, g_bias_one = jnp.sum(d_one * n_one, axis=0), jnp.sum(d_one, axis=0)
    grad_tokens = (grad_middle + norm_back(d_one, n_one, r_one, gain_f1)).astype(bf16)

    vector_grads = jnp.stack([g_gain_one, g_bias_one, g_gain_two, g_bias_two]).reshape(4, 4, 160)
    vector_grads = jnp.pad(vector_grads.transpose(1, 0, 2).reshape(4, 1, 640), ((0, 0), (0, 31), (0, 0))).astype(bf16)
    wide = jnp.pad(g_qkv, ((0, 0), (0, 128))).reshape(4, 160, 2, 640).transpose(0, 2, 1, 3).reshape(4, 320, 640)
    second = jnp.concatenate([wide, vector_grads], axis=1)
    second = summed_share(second, "batch")
    first = jnp.pad(first, ((0, 1536 - first.shape[0]), (0, 0)))
    second = jnp.pad(second, ((0, 512 - second.shape[0]), (0, 0)))
    first, second = summed_over_chips(first), summed_over_chips(second)
    total = jnp.concatenate([first[:1440], second[:336]])
    other = swapped(total)
    total, other = total.astype(f32), other.astype(f32)
    one, two = jnp.where(core == 0, total, other), jnp.where(core == 0, other, total)
    grad_up = jnp.stack([one[:640].reshape(4, 160, 640), two[:640].reshape(4, 160, 640)], axis=1)
    grad_up = grad_up.transpose(2, 0, 1, 3).reshape(160, 5120)
    grad_down = jnp.concatenate([one[640:1280], two[640:1280]])
    both = one[1280:] + two[1280:]
    grad_out = both[:160]
    parts = [x[1440:1760].reshape(2, 160, 640).transpose(1, 0, 2).reshape(160, 1280) for x in (one, two)]
    columns = []
    for part in range(3):
        a, b = (x[:, 384 * part:384 * (part + 1)] for x in parts)
        columns += [a[:, :256], b[:, :256], a[:, 256:] + b[:, 256:]]
    grad_qkv = jnp.concatenate(columns, axis=1)
    vectors = both[480].reshape(4, 160)
    return (
        block_out.reshape(2, 1, 256, 640), grad_tokens.reshape(2, 1, 256, 640), vectors[0], vectors[1], grad_qkv, grad_out,
        vectors[2], vectors[3], grad_up, grad_down)


def solution(mesh):
    fine = Mesh(mesh.devices.reshape(4, 4, 4, 2), ("batch", "z", "x", "core"))
    rows = P(None, "batch", ("z", "x", "core"), None)
    one, two = P("batch"), P("batch", None)
    return jax.shard_map(
        body,
        mesh=fine,
        in_specs=(rows, P(None, "batch", None), one, one, two, two, one, one, two, two, rows),
        out_specs=(rows, rows, one, one, two, two, one, one, two, two),
        check_vma=False,
    )
```

time: 1050 us -> 539 us (0.51)
  matrix products: 344 us -> 12.4 us
  waiting for transfers between devices: 309 us -> 128 us
  Pallas kernels: 0 us -> 109 us
  blocking collectives: 94.2 us -> 0 us
  other arithmetic: 75.2 us -> 34.7 us
  starting transfers between devices: 121 us -> 153 us
    dot_general x94 -> x8, matrix products: 344 us -> 12.4 us  [the longest x1 3.31 us: body(): lax.dot_general(hidden_all, flat, (((0,), (0,)), ((), ())), preferred_ele...]
    reduce_scatter x4 -> x1, waiting for transfers between devices: 154 us -> 0.02 us  [body(): lax.psum_scatter(first, 'batch', scatter_dimension=0, tiled=True)]
    pallas_call x0 -> x7, Pallas kernels: none -> 109 us  [the longest x2 34.7 us: attend_back(): pl.pallas_call(attend_back_kernel, out_shape=(jax.ShapeDtypeStruct((nq, 3...]
    psum x1 -> x0, blocking collectives: 65 us -> none  [body(): lax.psum(gradients[0].astype(jnp.bfloat16), 'seq').astype(jnp.float32)]
    psum x1 -> x0, waiting for transfers between devices: 34.4 us -> none  [body(): lax.psum(gradients[2].astype(jnp.bfloat16), 'seq').astype(jnp.float32)]
    ppermute x32 -> x54, starting transfers between devices: 120 us -> 153 us  [the longest x16 71.6 us: passed_along(): lax.ppermute(array, ('z', 'x'), [(i, i + by) for i in range(devices) if 0...]
    slice x14 -> x15, local copies, waits for them, and re-layouts: 33.8 us -> 10.2 us  [the longest x2 1.96 us: body(): pieces[2 + by]]
    reduce_sum x20 -> x5, other arithmetic: 27.7 us -> 5.07 us  [the longest x1 2.74 us: body(): jnp.sum(d_one * n_one, axis=0)]
  transfers between devices with their start and end apart: 40 -> 57, of which waited for: 19 -> 29; matrix products, arithmetic and copies ran while one was open for 34% -> 13% of each run, Pallas kernels for 0% -> 15%
where the time goes in v1:
time: 539 us; the launch traced here: 528 us
  starting transfers between devices  153 us (28%)
  waiting for transfers between devices  128 us (24%)
  Pallas kernels  109 us (20%)
  local copies, waits for them, and re-layouts  70.3 us (13%)
  other arithmetic  34.7 us (6%)
  between operations  21.1 us (4%)
  matrix products  12.4 us (2%)
    ppermute x16, starting transfers between devices, passed_along(): lax.ppermute(array, ('z', 'x'), [(i, i + by) for i in range(devices) if 0...  71.6 us
    ppermute x30, waiting for transfers between devices, shifted(): lax.ppermute(array, axis, [(i, (i + by) % devices) for i in range(devices)])  61.1 us
    ppermute x16, waiting for transfers between devices, passed_along(): lax.ppermute(array, ('z', 'x'), [(i, i + by) for i in range(devices) if 0...  60.4 us
    ppermute x30, starting transfers between devices, shifted(): lax.ppermute(array, axis, [(i, (i + by) % devices) for i in range(devices)])  50.8 us
    pallas_call x2, Pallas kernels, attend_back(): pl.pallas_call(attend_back_kernel, out_shape=(jax.ShapeDtypeStruct((nq, 3...  34.7 us
    pallas_call x1, Pallas kernels, feed_forward(): pl.pallas_call(feed_kernel, out_shape=(jax.ShapeDtypeStruct((rows, 640),...  32.5 us
    ppermute x8, starting transfers between devices, swapped(): return lax.ppermute(array, 'core', [(0, 1), (1, 0)])  30.5 us
    unnamed x142, local copies, waits for them, and re-layouts  24.3 us
  transfers between devices with their start and end apart: 57, of which 29 were waited for; matrix products, arithmetic and copies ran while one was open for 13% of the time, Pallas kernels for 15%

profile of v1, /device:TPU:1, one launch (start us, length us, event | category | flops | bytes accessed | tf_op | source)
XLA Modules:
  0.0 528.5 jit_solution(17323981307760598356)
XLA Ops:
  16.7 5.4 %collective-permute-start.8 = (bf16[256,640]{1,0:T(8,128)(2,1)}, bf16[256,640]{1,0:T(8,128)(2,1)}, u32[]{:S(2)}, u32[]{:S(2)}) collective-permute-start(bf16[256,640]{1,0:T(8,128)(2,1)} %get-tuple-element.156), channel_id=1, source_target_pairs={{0,4},{2,6},{4,8},{6,10},{8,12},{10,14},{12,16},{14,18},{16,20},{1... | collective-permute-start | bytes 983048 | tf_op jit(solution)/shard_map/ppermute | solution.py:356
  29.8 5.1 dynamic-slice_reduce_fusion
  55.2 5.5 %collective-permute-done.1 = bf16[256,640]{1,0:T(8,128)(2,1)S(1)} collective-permute-done((bf16[256,640]{1,0:T(8,128)(2,1)}, bf16[256,640]{1,0:T(8,128)(2,1)S(1)}, u32[]{:S(2)}, u32[]{:S(2)}) %collective-permute-start.1) | collective-permute-done | bytes 327712 | tf_op jit(solution)/shard_map/ppermute | solution.py:356
  64.3 6.4 %collective-permute-done.11 = bf16[256,640]{1,0:T(8,128)(2,1)S(1)} collective-permute-done((bf16[256,640]{1,0:T(8,128)(2,1)}, bf16[256,640]{1,0:T(8,128)(2,1)S(1)}, u32[]{:S(2)}, u32[]{:S(2)}) %collective-permute-start.11) | collective-permute-done | bytes 327712 | tf_op jit(solution)/shard_map/ppermute | solution.py:356
  72.1 12.4 %collective-permute-start.12 = (bf16[5,256,640]{2,1,0:T(8,128)(2,1)S(1)}, bf16[5,256,640]{2,1,0:T(8,128)(2,1)S(1)}, u32[]{:S(2)}, u32[]{:S(2)}) collective-permute-start(bf16[5,256,640]{2,1,0:T(8,128)(2,1)S(1)} %bitcast_dynamic-update-slice_fusion.8.own_ref), channel_id=1, source_target_pairs={{0,1},{1,0},{2,3},{3,2},{4,5},{5,4},{6,7},{7,6},{8,9},{9,8},{10,11... | collective-permute-start | bytes 4915208 | tf_op jit(solution)/shard_map/ppermute | solution.py:360
  92.5 9.8 %project.3 = (bf16[2560,384]{1,0:T(8,128)(2,1)}, bf16[2560,384]{1,0:T(8,128)(2,1)}, bf16[384,2560]{1,0:T(8,128)(2,1)}, bf16[384,2560]{1,0:T(8,128)(2,1)}, bf16[5...) custom-call(s32[1]{0:T(128)} %bitcast.2.core_ref, ...), custom_call_target="tpu_custom_call" | custom-call | flops 5000000000 | bytes 12582912 | tf_op jit(solution)/shard_map/project/pallas_call | solution.py:261
  104.0 12.2 %attend.3 = (f32[384,512]{1,0:T(8,128)S(1)}, bf16[512,384]{1,0:T(8,128)(2,1)S(1)}, f32[5,8,512]{2,1,0:T(8,128)S(1)}) custom-call(s32[5]{0:T(128)S(1)} %stack.163.info_ref, bf16[384,512]{1,0:T(8,128)(2,1)S(1)} %get-tuple-element.44.qT_ref, bf16[2560,384]{1,0:T(8,128)(2,1)S(1)} %copy-done.4, bf16[384,2560]{1,0:T(8,128)(2,1)} %get-tuple-element.46.vT_ref, ...), custom_call_target="tpu_custom_call" | custom-call | flops 20000000000 | bytes 6291456 | tf_op jit(solution)/shard_map/attend/pallas_call | solution.py:102
  116.3 9.8 %project.2 = (bf16[2560,384]{1,0:T(8,128)(2,1)}, bf16[2560,384]{1,0:T(8,128)(2,1)}, bf16[384,2560]{1,0:T(8,128)(2,1)}, bf16[384,2560]{1,0:T(8,128)(2,1)}, bf16[5...) custom-call(s32[1]{0:T(128)} %bitcast.2.core_ref, ...), custom_call_target="tpu_custom_call" | custom-call | flops 5000000000 | bytes 12582912 | tf_op jit(solution)/shard_map/project/pallas_call | solution.py:261
  128.2 10.2 %attend.2 = (f32[384,512]{1,0:T(8,128)S(1)}, bf16[512,384]{1,0:T(8,128)(2,1)S(1)}, f32[5,8,512]{2,1,0:T(8,128)S(1)}) custom-call(s32[5]{0:T(128)S(1)} %stack.147.info_ref, bf16[384,512]{1,0:T(8,128)(2,1)S(1)} %get-tuple-element.40.qT_ref, bf16[2560,384]{1,0:T(8,128)(2,1)S(1)} %copy-done.5, bf16[384,2560]{1,0:T(8,128)(2,1)} %get-tuple-element.42.vT_ref, ...), custom_call_target="tpu_custom_call" | custom-call | flops 20000000000 | bytes 6291456 | tf_op jit(solution)/shard_map/attend/pallas_call | solution.py:102
  153.3 32.5 %feed_forward.1 = (f32[1024,640]{1,0:T(8,128)}, f32[1024,640]{1,0:T(8,128)}, bf16[4,640,640]{2,1,0:T(8,128)(2,1)}, bf16[4,640,640]{2,1,0:T(8,128)(2,1)}) custom-call(bf16[1024,640]{1,0:T(8,128)(2,1)} %get-tuple-element.191.h_ref, bf16[1024,640]{1,0:T(8,128)(2,1)} %get-tuple-element.192.cot_ref, bf16[640,2560]{1,0:T(8,128)(2,1)} %all-gather.3.cloned.1.call-done.up_ref, ...), custom_call_target="tpu_custom_call" | custom-call | flops 20000000000 | bytes 31457280 | tf_op jit(solution)/shard_map/feed_forward/pallas_call | solution.py:323
  209.6 15.8 %attend_back.2 = (bf16[512,384]{1,0:T(8,128)(2,1)S(1)}, bf16[2560,384]{1,0:T(8,128)(2,1)S(1)}, bf16[2560,384]{1,0:T(8,128)(2,1)}) custom-call(s32[5]{0:T(128)S(1)} %stack.147.info_ref, bf16[384,512]{1,0:T(8,128)(2,1)S(1)} %copy-done.11, bf16[512,384]{1,0:T(8,128)(2,1)S(1)} %copy-done.9, bf16[2560,384]{1,0:T(8,128)(2,1)} %get-tuple-element.41.k_ref, ...), custom_call_target="tpu_custom_call" | custom-call | flops 40000000000 | bytes 12582912 | tf_op jit(solution)/shard_map/attend_back/pallas_call | solution.py:215
  229.1 11.4 %collective-permute-start.17 = (bf16[512,768]{1,0:T(8,128)(2,1)}, bf16[512,768]{1,0:T(8,128)(2,1)S(1)}, u32[]{:S(2)}, u32[]{:S(2)}) collective-permute-start(bf16[512,768]{1,0:T(8,128)(2,1)} %get-tuple-element.126), channel_id=1, source_target_pairs={{0,2},{2,4},{4,6},{6,8},{8,10},{10,12},{12,14},{14,16},{16,18},{18... | collective-permute-start | bytes 2359304 | tf_op jit(solution)/shard_map/ppermute | solution.py:356
  241.8 15.1 %collective-permute-start.19 = (bf16[512,768]{1,0:T(8,128)(2,1)}, bf16[512,768]{1,0:T(8,128)(2,1)}, u32[]{:S(2)}, u32[]{:S(2)}) collective-permute-start(bf16[512,768]{1,0:T(8,128)(2,1)} %get-tuple-element.128), channel_id=1, source_target_pairs={{0,4},{2,6},{4,8},{6,10},{8,12},{10,14},{12,16},{14,18},{16,20},{1... | collective-permute-start | bytes 2359304 | tf_op jit(solution)/shard_map/ppermute | solution.py:356
  260.2 18.9 %attend_back.3 = (bf16[512,384]{1,0:T(8,128)(2,1)S(1)}, bf16[2560,384]{1,0:T(8,128)(2,1)S(1)}, bf16[2560,384]{1,0:T(8,128)(2,1)}) custom-call(s32[5]{0:T(128)S(1)} %stack.163.info_ref, bf16[384,512]{1,0:T(8,128)(2,1)S(1)} %copy-done.7, bf16[512,384]{1,0:T(8,128)(2,1)S(1)} %get-tuple-element.56.q_ref, bf16[2560,384]{1,0:T(8,128)(2,1)} %get-tuple-element.45.k_ref, ...), custom_call_target="tpu_custom_call" | custom-call | flops 40000000000 | bytes 12582912 | tf_op jit(solution)/shard_map/attend_back/pallas_call | solution.py:215
  281.2 10.3 %collective-permute-start.21 = (bf16[512,768]{1,0:T(8,128)(2,1)S(1)}, bf16[512,768]{1,0:T(8,128)(2,1)S(1)}, u32[]{:S(2)}, u32[]{:S(2)}) collective-permute-start(bf16[512,768]{1,0:T(8,128)(2,1)S(1)} %get-tuple-element.130), channel_id=1, source_target_pairs={{0,2},{2,4},{4,6},{6,8},{8,10},{10,12},{12,14},{14,16},{16,18},{18... | collective-permute-start | bytes 2359304 | tf_op jit(solution)/shard_map/ppermute | solution.py:356
  292.9 9.7 %collective-permute-start.23 = (bf16[512,768]{1,0:T(8,128)(2,1)S(1)}, bf16[512,768]{1,0:T(8,128)(2,1)S(1)}, u32[]{:S(2)}, u32[]{:S(2)}) collective-permute-start(bf16[512,768]{1,0:T(8,128)(2,1)S(1)} %get-tuple-element.132), channel_id=1, source_target_pairs={{0,4},{2,6},{4,8},{6,10},{8,12},{10,14},{12,16},{14,18},{16,20},{1... | collective-permute-start | bytes 2359304 | tf_op jit(solution)/shard_map/ppermute | solution.py:356
  311.2 13.0 %collective-permute-done.23 = bf16[512,768]{1,0:T(8,128)(2,1)S(1)} collective-permute-done((bf16[512,768]{1,0:T(8,128)(2,1)S(1)}, bf16[512,768]{1,0:T(8,128)(2,1)S(1)}, u32[]{:S(2)}, u32[]{:S(2)}) %collective-permute-start.23) | collective-permute-done | bytes 786464 | tf_op jit(solution)/shard_map/ppermute | solution.py:356
  324.2 29.2 %collective-permute-done.24 = bf16[512,768]{1,0:T(8,128)(2,1)S(1)} collective-permute-done((bf16[512,768]{1,0:T(8,128)(2,1)S(1)}, bf16[512,768]{1,0:T(8,128)(2,1)S(1)}, u32[]{:S(2)}, u32[]{:S(2)}) %collective-permute-start.24) | collective-permute-done | bytes 786464 | tf_op jit(solution)/shard_map/ppermute | solution.py:356
  376.9 20.1 %collective-permute-done.38 = bf16[352,640]{1,0:T(8,128)(2,1)S(1)} collective-permute-done((bf16[352,640]{1,0:T(8,128)(2,1)}, bf16[352,640]{1,0:T(8,128)(2,1)S(1)}, u32[]{:S(2)}, u32[]{:S(2)}) %collective-permute-start.38) | collective-permute-done | bytes 450592 | tf_op jit(solution)/shard_map/ppermute | solution.py:351
  398.4 12.4 %collective-permute-start.41 = (bf16[128,640]{1,0:T(8,128)(2,1)S(1)}, bf16[128,640]{1,0:T(8,128)(2,1)S(1)}, u32[]{:S(2)}, u32[]{:S(2)}) collective-permute-start(bf16[128,640]{1,0:T(8,128)(2,1)S(1)} %get-tuple-element.151), channel_id=1, source_target_pairs={{0,8},{8,16},{16,24},{24,0},{1,9},{9,17},{17,25},{25,1},{2,10},{10... | collective-permute-start | bytes 491528 | tf_op jit(solution)/shard_map/ppermute | solution.py:351
  441.6 10.8 %collective-permute-done.28 = bf16[384,640]{1,0:T(8,128)(2,1)S(1)} collective-permute-done((bf16[384,640]{1,0:T(8,128)(2,1)S(1)}, bf16[384,640]{1,0:T(8,128)(2,1)S(1)}, u32[]{:S(2)}, u32[]{:S(2)}) %collective-permute-start.28) | collective-permute-done | bytes 491552 | tf_op jit(solution)/shard_map/ppermute | solution.py:351
  474.3 9.8 %collective-permute-done.35 = bf16[384,640]{1,0:T(8,128)(2,1)S(1)} collective-permute-done((bf16[384,640]{1,0:T(8,128)(2,1)S(1)}, bf16[384,640]{1,0:T(8,128)(2,1)S(1)}, u32[]{:S(2)}, u32[]{:S(2)}) %collective-permute-start.35) | collective-permute-done | bytes 491552 | tf_op jit(solution)/shard_map/ppermute | solution.py:351
  485.9 10.5 %collective-permute-start.53 = (bf16[1776,640]{1,0:T(8,128)(2,1)S(1)}, bf16[1776,640]{1,0:T(8,128)(2,1)S(1)}, u32[]{:S(2)}, u32[]{:S(2)}) collective-permute-start(bf16[1776,640]{1,0:T(8,128)(2,1)S(1)} %pad_maximum_fusion.2), channel_id=1, source_target_pairs={{0,1},{1,0},{2,3},{3,2},{4,5},{5,4},{6,7},{7,6},{8,9},{9,8},{10,11... | collective-permute-start | bytes 6819848 | tf_op jit(solution)/shard_map/ppermute | solution.py:360
  510.8 5.6 %reshape.431 = f32[160,5120]{1,0:T(8,128)} reshape(f32[160,4,2,640]{3,2,1,0:T(2,128)} %copy.40) | data formatting | bytes 6553600 | tf_op jit(solution)/shard_map/reshape | solution.py:510
  (396 shorter events, 205.4 us)
Async XLA Ops:
  7.2 146.1 %all-gather.5.cloned.1.call-start = ((), (), s32[]{:S(2)}) async-start(), calls=%async_computation.2 | async-start | bytes 4096000 | tf_op jit(solution)/shard_map/all_gather | solution.py:435
  9.6 143.7 %all-gather.3.cloned.1.call-start = ((), (), s32[]{:S(2)}) async-start(), calls=%async_computation.1 | async-start | bytes 4096000 | tf_op jit(solution)/shard_map/all_gather | solution.py:434
  10.6 78.1 %collective-permute-start.5 = (bf16[160,1920]{1,0:T(8,128)(2,1)S(1)}, bf16[160,1920]{1,0:T(8,128)(2,1)}, u32[]{:S(2)}, u32[]{:S(2)}) collective-permute-start(bf16[160,1920]{1,0:T(8,128)(2,1)S(1)} %constant_dynamic-update-slice_fusion), channel_id=1, source_target_pairs={{0,32},{32,64},{64,96},{96,0},{1,33},{33,65},{65,97},{97,1},{2,34}... | collective-permute-start | bytes 1843208 | tf_op jit(solution)/shard_map/ppermute | solution.py:351
  12.8 77.1 %collective-permute-start.6 = (bf16[160,1920]{1,0:T(8,128)(2,1)S(1)}, bf16[160,1920]{1,0:T(8,128)(2,1)}, u32[]{:S(2)}, u32[]{:S(2)}) collective-permute-start(bf16[160,1920]{1,0:T(8,128)(2,1)S(1)} %constant_dynamic-update-slice_fusion), channel_id=1, source_target_pairs={{0,96},{32,0},{64,32},{96,64},{1,97},{33,1},{65,33},{97,65},{2,98}... | collective-permute-start | bytes 1843208 | tf_op jit(solution)/shard_map/ppermute | solution.py:351
  14.3 76.7 %collective-permute-start.7 = (bf16[160,1920]{1,0:T(8,128)(2,1)S(1)}, bf16[160,1920]{1,0:T(8,128)(2,1)S(1)}, u32[]{:S(2)}, u32[]{:S(2)}) collective-permute-start(bf16[160,1920]{1,0:T(8,128)(2,1)S(1)} %constant_dynamic-update-slice_fusion), channel_id=1, source_target_pairs={{0,64},{32,96},{64,0},{96,32},{1,65},{33,97},{65,1},{97,33},{2,66}... | collective-permute-start | bytes 1843208 | tf_op jit(solution)/shard_map/ppermute | solution.py:351
  16.7 28.6 %collective-permute-start.8 = (bf16[256,640]{1,0:T(8,128)(2,1)}, bf16[256,640]{1,0:T(8,128)(2,1)}, u32[]{:S(2)}, u32[]{:S(2)}) collective-permute-start(bf16[256,640]{1,0:T(8,128)(2,1)} %get-tuple-element.156), channel_id=1, source_target_pairs={{0,4},{2,6},{4,8},{6,10},{8,12},{10,14},{12,16},{14,18},{16,20},{1... | collective-permute-start | bytes 983048 | tf_op jit(solution)/shard_map/ppermute | solution.py:356
  22.2 27.3 %collective-permute-start = (bf16[256,640]{1,0:T(8,128)(2,1)}, bf16[256,640]{1,0:T(8,128)(2,1)}, u32[]{:S(2)}, u32[]{:S(2)}) collective-permute-start(bf16[256,640]{1,0:T(8,128)(2,1)} %get-tuple-element.157), channel_id=1, source_target_pairs={{0,4},{2,6},{4,8},{6,10},{8,12},{10,14},{12,16},{14,18},{16,20},{1... | collective-permute-start | bytes 983048 | tf_op jit(solution)/shard_map/ppermute | solution.py:356
  36.0 391.8 %reduce-scatter.2.cloned.1.call-start = ((), (), s32[]{:S(2)}) async-start(), calls=%async_computation.3 | async-start | bytes 9216000 | tf_op jit(solution)/shard_map/reduce_scatter | solution.py:470
  72.1 20.4 %collective-permute-start.12 = (bf16[5,256,640]{2,1,0:T(8,128)(2,1)S(1)}, bf16[5,256,640]{2,1,0:T(8,128)(2,1)S(1)}, u32[]{:S(2)}, u32[]{:S(2)}) collective-permute-start(bf16[5,256,640]{2,1,0:T(8,128)(2,1)S(1)} %bitcast_dynamic-update-slice_fusion.8.own_ref), channel_id=1, source_target_pairs={{0,1},{1,0},{2,3},{3,2},{4,5},{5,4},{6,7},{7,6},{8,9},{9,8},{10,11... | collective-permute-start | bytes 4915208 | tf_op jit(solution)/shard_map/ppermute | solution.py:360
  84.6 31.6 %collective-permute-start.4 = (bf16[5,256,640]{2,1,0:T(8,128)(2,1)S(1)}, bf16[5,256,640]{2,1,0:T(8,128)(2,1)S(1)}, u32[]{:S(2)}, u32[]{:S(2)}) collective-permute-start(bf16[5,256,640]{2,1,0:T(8,128)(2,1)S(1)} %bitcast_dynamic-update-slice_fusion.13.own_ref), channel_id=1, source_target_pairs={{0,1},{1,0},{2,3},{3,2},{4,5},{5,4},{6,7},{7,6},{8,9},{9,8},{10,11... | collective-permute-start | bytes 4915208 | tf_op jit(solution)/shard_map/ppermute | solution.py:360
  229.1 62.4 %collective-permute-start.17 = (bf16[512,768]{1,0:T(8,128)(2,1)}, bf16[512,768]{1,0:T(8,128)(2,1)S(1)}, u32[]{:S(2)}, u32[]{:S(2)}) collective-permute-start(bf16[512,768]{1,0:T(8,128)(2,1)} %get-tuple-element.126), channel_id=1, source_target_pairs={{0,2},{2,4},{4,6},{6,8},{8,10},{10,12},{12,14},{14,16},{16,18},{18... | collective-permute-start | bytes 2359304 | tf_op jit(solution)/shard_map/ppermute | solution.py:356
  240.5 52.4 %collective-permute-start.18 = (bf16[512,768]{1,0:T(8,128)(2,1)}, bf16[512,768]{1,0:T(8,128)(2,1)}, u32[]{:S(2)}, u32[]{:S(2)}) collective-permute-start(bf16[512,768]{1,0:T(8,128)(2,1)} %get-tuple-element.129), channel_id=1, source_target_pairs={{2,0},{4,2},{6,4},{8,6},{10,8},{12,10},{14,12},{16,14},{18,16},{20... | collective-permute-start | bytes 2359304 | tf_op jit(solution)/shard_map/ppermute | solution.py:356
  241.8 60.8 %collective-permute-start.19 = (bf16[512,768]{1,0:T(8,128)(2,1)}, bf16[512,768]{1,0:T(8,128)(2,1)}, u32[]{:S(2)}, u32[]{:S(2)}) collective-permute-start(bf16[512,768]{1,0:T(8,128)(2,1)} %get-tuple-element.128), channel_id=1, source_target_pairs={{0,4},{2,6},{4,8},{6,10},{8,12},{10,14},{12,16},{14,18},{16,20},{1... | collective-permute-start | bytes 2359304 | tf_op jit(solution)/shard_map/ppermute | solution.py:356
  256.9 47.2 %collective-permute-start.20 = (bf16[512,768]{1,0:T(8,128)(2,1)}, bf16[512,768]{1,0:T(8,128)(2,1)}, u32[]{:S(2)}, u32[]{:S(2)}) collective-permute-start(bf16[512,768]{1,0:T(8,128)(2,1)} %get-tuple-element.127), channel_id=1, source_target_pairs={{4,0},{6,2},{8,4},{10,6},{12,8},{14,10},{16,12},{18,14},{20,16},{2... | collective-permute-start | bytes 2359304 | tf_op jit(solution)/shard_map/ppermute | solution.py:356
  281.2 26.1 %collective-permute-start.21 = (bf16[512,768]{1,0:T(8,128)(2,1)S(1)}, bf16[512,768]{1,0:T(8,128)(2,1)S(1)}, u32[]{:S(2)}, u32[]{:S(2)}) collective-permute-start(bf16[512,768]{1,0:T(8,128)(2,1)S(1)} %get-tuple-element.130), channel_id=1, source_target_pairs={{0,2},{2,4},{4,6},{6,8},{8,10},{10,12},{12,14},{14,16},{16,18},{18... | collective-permute-start | bytes 2359304 | tf_op jit(solution)/shard_map/ppermute | solution.py:356
  291.6 19.6 %collective-permute-start.22 = (bf16[512,768]{1,0:T(8,128)(2,1)S(1)}, bf16[512,768]{1,0:T(8,128)(2,1)S(1)}, u32[]{:S(2)}, u32[]{:S(2)}) collective-permute-start(bf16[512,768]{1,0:T(8,128)(2,1)S(1)} %get-tuple-element.133), channel_id=1, source_target_pairs={{2,0},{4,2},{6,4},{8,6},{10,8},{12,10},{14,12},{16,14},{18,16},{20... | collective-permute-start | bytes 2359304 | tf_op jit(solution)/shard_map/ppermute | solution.py:356
  292.9 31.3 %collective-permute-start.23 = (bf16[512,768]{1,0:T(8,128)(2,1)S(1)}, bf16[512,768]{1,0:T(8,128)(2,1)S(1)}, u32[]{:S(2)}, u32[]{:S(2)}) collective-permute-start(bf16[512,768]{1,0:T(8,128)(2,1)S(1)} %get-tuple-element.132), channel_id=1, source_target_pairs={{0,4},{2,6},{4,8},{6,10},{8,12},{10,14},{12,16},{14,18},{16,20},{1... | collective-permute-start | bytes 2359304 | tf_op jit(solution)/shard_map/ppermute | solution.py:356
  302.6 50.7 %collective-permute-start.24 = (bf16[512,768]{1,0:T(8,128)(2,1)S(1)}, bf16[512,768]{1,0:T(8,128)(2,1)S(1)}, u32[]{:S(2)}, u32[]{:S(2)}) collective-permute-start(bf16[512,768]{1,0:T(8,128)(2,1)S(1)} %get-tuple-element.131), channel_id=1, source_target_pairs={{4,0},{6,2},{8,4},{10,6},{12,8},{14,10},{16,12},{18,14},{20,16},{2... | collective-permute-start | bytes 2359304 | tf_op jit(solution)/shard_map/ppermute | solution.py:356
  374.2 22.8 %collective-permute-start.38 = (bf16[352,640]{1,0:T(8,128)(2,1)}, bf16[352,640]{1,0:T(8,128)(2,1)S(1)}, u32[]{:S(2)}, u32[]{:S(2)}) collective-permute-start(bf16[352,640]{1,0:T(8,128)(2,1)} %get-tuple-element.138), channel_id=1, source_target_pairs={{0,32},{32,64},{64,96},{96,0},{1,33},{33,65},{65,97},{97,1},{2,34}... | collective-permute-start | bytes 1351688 | tf_op jit(solution)/shard_map/ppermute | solution.py:351
  374.2 22.8 %collective-permute-start.39 = (bf16[352,640]{1,0:T(8,128)(2,1)}, bf16[352,640]{1,0:T(8,128)(2,1)S(1)}, u32[]{:S(2)}, u32[]{:S(2)}) collective-permute-start(bf16[352,640]{1,0:T(8,128)(2,1)} %get-tuple-element.140), channel_id=1, source_target_pairs={{0,96},{32,0},{64,32},{96,64},{1,97},{33,1},{65,33},{97,65},{2,98}... | collective-permute-start | bytes 1351688 | tf_op jit(solution)/shard_map/ppermute | solution.py:351
  376.9 20.1 %collective-permute-start.40 = (bf16[352,640]{1,0:T(8,128)(2,1)}, bf16[352,640]{1,0:T(8,128)(2,1)}, u32[]{:S(2)}, u32[]{:S(2)}) collective-permute-start(bf16[352,640]{1,0:T(8,128)(2,1)} %get-tuple-element.139), channel_id=1, source_target_pairs={{0,64},{32,96},{64,0},{96,32},{1,65},{33,97},{65,1},{97,33},{2,66}... | collective-permute-start | bytes 1351688 | tf_op jit(solution)/shard_map/ppermute | solution.py:351
  398.4 14.7 %collective-permute-start.41 = (bf16[128,640]{1,0:T(8,128)(2,1)S(1)}, bf16[128,640]{1,0:T(8,128)(2,1)S(1)}, u32[]{:S(2)}, u32[]{:S(2)}) collective-permute-start(bf16[128,640]{1,0:T(8,128)(2,1)S(1)} %get-tuple-element.151), channel_id=1, source_target_pairs={{0,8},{8,16},{16,24},{24,0},{1,9},{9,17},{17,25},{25,1},{2,10},{10... | collective-permute-start | bytes 491528 | tf_op jit(solution)/shard_map/ppermute | solution.py:351
  433.9 18.6 %collective-permute-start.28 = (bf16[384,640]{1,0:T(8,128)(2,1)S(1)}, bf16[384,640]{1,0:T(8,128)(2,1)S(1)}, u32[]{:S(2)}, u32[]{:S(2)}) collective-permute-start(bf16[384,640]{1,0:T(8,128)(2,1)S(1)} %get-tuple-element.136), channel_id=1, source_target_pairs={{0,16},{8,24},{16,0},{24,8},{1,17},{9,25},{17,1},{25,9},{2,18},{10... | collective-permute-start | bytes 1474568 | tf_op jit(solution)/shard_map/ppermute | solution.py:351
  437.6 20.2 %collective-permute-start.49 = (bf16[32,640]{1,0:T(8,128)(2,1)S(1)}, bf16[32,640]{1,0:T(8,128)(2,1)S(1)}, u32[]{:S(2)}, u32[]{:S(2)}) collective-permute-start(bf16[32,640]{1,0:T(8,128)(2,1)S(1)} %get-tuple-element.113), channel_id=1, source_target_pairs={{0,4},{2,6},{4,0},{6,2},{1,5},{3,7},{5,1},{7,3},{8,12},{10,14},{12... | collective-permute-start | bytes 122888 | tf_op jit(solution)/shard_map/ppermute | solution.py:351
  (90 other events, 518.3 us)
Sparse Core Ops, SparseCore 0:
  10.3 58.0 all-gather.4
  70.7 42.6 all-gather.2
  206.5 86.2 reduce-scatter.1
